TPU v7x, 128 devices: a whole 4x4x4 slice. The times are simulated.
128 devices in a mesh: dp: 16 (over x_hi, y, core), cores: 8 (over z, x_lo).
Axes of the slice: x: 4 (x_hi: 2, x_lo: 2; x = x_hi * 2 + x_lo), y: 4, z: 4, core: 2. Of those that a mesh axis runs over, the one named last changes fastest.
Arguments:
- data: bfloat16 [65536, 768], P('dp'), may hold values from -6 to 6
- data_pot: bfloat16 [65536], P('dp'), may hold values from -6 to 6
- coreset: bfloat16 [4096, 768], P('cores')
- core_pot: bfloat16 [4096], P('cores'), may hold values from -12 to 12
Outputs:
- core_grad: float32 [4096, 768], P('cores', 'dp')
All inputs are finite; a program needn't handle non-finite values.
Results may differ from a plain program's by a relative error of at most 0.0095.
Values may be sent and summed in bfloat16 or wider, within the bound.
No kernel may reach another device: no remote copies, remote signals or barrier semaphores. Data moves between devices by JAX's collectives and lax.ppermute only.
A program may use at most 128 MiB of HBM per device.

v0:
```python
import math

import jax
import jax.numpy as jnp
from jax import lax
from jax.sharding import PartitionSpec as P


def joined(value, axis, combine):
    everything = jax.tree.map(lambda part: lax.all_gather(part, axis), value)
    leading = jax.tree.map(lambda part: part[0], everything)

    def turn(k, so_far):
        return combine(so_far, jax.tree.map(lambda part: part[k], everything))

    return lax.fori_loop(1, lax.axis_size(axis), turn, leading)


def combine_parts(first, second):
    top = jnp.maximum(first[0], second[0])
    left = jnp.exp(first[0] - top)
    right = jnp.exp(second[0] - top)
    return (
        top,
        first[1] * left + second[1] * right,
        first[2] * left[:, None] + second[2] * right[:, None],
    )


def on_device(data, data_pot, coreset, core_pot):
    scale = 30.0 / math.sqrt(data.shape[1])
    width_all = data.shape[1]
    position = lax.axis_index("dp")
    count_dp = lax.axis_size("dp")
    width = width_all // count_dp
    query = coreset.shape[0] // count_dp
    scores = data_pot.astype(jnp.float32)[None, :] + scale * lax.dot_general(
        coreset, data, (((1,), (1,)), ((), ())), preferred_element_type=jnp.float32
    )
    top = jnp.max(scores, axis=1)
    weights = jnp.exp(scores - top[:, None]).astype(jnp.bfloat16)
    total = jnp.sum(weights.astype(jnp.float32), axis=1)
    summed = jnp.dot(weights, data, preferred_element_type=jnp.float32)
    merged = joined((top, total, summed), "dp", combine_parts)
    columns = lax.dynamic_slice_in_dim(merged[2], position * width, width, 1)
    pull = columns / merged[1][:, None]
    queries = lax.dynamic_slice_in_dim(coreset, position * query, query, 0)
    start_state = (
        jnp.full((query,), -1e30, jnp.float32),
        jnp.zeros((query,), jnp.float32),
        jnp.zeros((query, width_all), jnp.float32),
    )
    keys = lax.all_gather(coreset, "cores", axis=0, tiled=True)
    potential = lax.all_gather(core_pot, "cores", axis=0, tiled=True)
    block_scores = potential.astype(jnp.float32)[None, :] + scale * lax.dot_general(
        queries, keys, (((1,), (1,)), ((), ())), preferred_element_type=jnp.float32
    )
    new_top = jnp.maximum(start_state[0], jnp.max(block_scores, axis=1))
    block_weights = jnp.exp(block_scores - new_top[:, None]).astype(jnp.bfloat16)
    new_total = jnp.sum(block_weights.astype(jnp.float32), axis=1)
    new_sum = jnp.dot(block_weights, keys, preferred_element_type=jnp.float32)
    self_rows = new_sum / new_total[:, None]
    push = lax.all_to_all(
        self_rows.astype(jnp.bfloat16), "dp", split_axis=1, concat_axis=0, tiled=True
    ).astype(self_rows.dtype)
    return push - pull


def solution(mesh):
    return jax.shard_map(
        on_device,
        mesh=mesh,
        in_specs=(P("dp", None), P("dp"), P("cores", None), P("cores")),
        out_specs=P("cores", "dp"),
        check_vma=False,
    )
```

profile of v0, /device:TPU:1, one launch (start us, length us, event | category | flops | bytes accessed | tf_op | source)
XLA Modules:
  0.0 330.7 jit_solution(7514119079296244754)
XLA Ops:
  6.5 0.0 all-gather.9.cloned.1.call-start
  6.5 0.7 all-gather.9.cloned.1.call-update
  7.3 0.0 all-gather.11.cloned.1.call-start
  7.3 0.7 convert_element_type.37
  8.0 6.0 %fusion.1 = (f32[512]{0:T(512)S(1)}, f32[512,4096]{1,0:T(8,128)S(1)}) fusion(f32[4096]{0:T(1024)S(1)} %convert_element_type.37, bf16[512,768]{1,0:T(8,128)(2,1)} %param.8, bf16[4096,768]{1,0:T(8,128)(2,1)} %param.6), kind=kOutput, calls=%fused_computation.10 | convolution fusion | flops 3227516416 | bytes 15484928 | tf_op jit(solution)/shard_map/dot_general | solution.py:37
  14.0 0.0 copy-start.2
  14.0 2.7 convert_reduce_fusion
  16.6 0.1 copy-done.2
  16.8 0.0 copy-start.1
  16.8 4.6 %fusion.7 = f32[512,768]{1,0:T(8,128)} fusion(bf16[512,4096]{1,0:T(8,128)(2,1)S(1)} %get-tuple-element.203, bf16[4096,768]{1,0:T(8,128)(2,1)S(1)} %copy-done.2), kind=kOutput, calls=%fused_computation.26 | convolution fusion | flops 3221225472 | bytes 12058624 | tf_op jit(solution)/shard_map/dot_general | solution.py:43
  21.3 0.0 all-gather.11.cloned.1.call-update
  21.4 0.0 copy-done.1
  21.4 23.1 %all-gather.3 = bf16[8,1,512]{2,1,0:T(2,128)(2,1)S(1)} all-gather(bf16[1,1,512]{2,1,0:T(2,128)(2,1)S(1)} %reshape.25), channel_id=1, replica_groups=mesh['dp'=16,'cores'=8] {'cores'}, dimensions={0}, use_global_device_ids=true | all-gather | bytes 9216 | tf_op jit(solution)/shard_map/all_gather | solution.py:54
  44.5 97.3 %all-gather.9.cloned.1.call-done = bf16[4096,768]{1,0:T(8,128)(2,1)} async-done(((bf16[512,768]{1,0:T(8,128)(2,1)}), bf16[4096,768]{1,0:T(8,128)(2,1)}) %all-gather.9.cloned.1.call-update) | async-done | bytes 6291472 | tf_op jit(solution)/shard_map/all_gather | solution.py:53
  141.9 0.0 copy-start
  141.9 5.0 %fusion.6 = (f32[32]{0:T(128)S(1)}, f32[32,4096]{1,0:T(8,128)S(1)}) fusion(bf16[4096,768]{1,0:T(8,128)(2,1)} %all-gather.9.cloned.1.call-done, bf16[512,768]{1,0:T(8,128)(2,1)} %param.8, s32[]{:T(128)S(6)} %select_n.18, f32[4096]{0:T(1024)S(1)} %bitcast.45), kind=kOutput, calls=%fused_computation.23 | convolution fusion | flops 201719776 | bytes 6881412 | tf_op jit(solution)/shard_map/dot_general | solution.py:55
  146.9 0.3 convert_reduce_fusion.1
  147.1 0.0 copy-done
  147.1 1.2 fusion.3
  148.4 0.2 all_to_all.10
  148.6 0.8 reshape.36
  149.4 7.4 %all-to-all-start = ((bf16[16,2,768]{2,1,0:T(2,128)(2,1)}), bf16[16,2,768]{2,1,0:T(2,128)(2,1)S(1)}, u32[]{:S(2)}, u32[]{:S(2)}) async-start(bf16[16,2,768]{2,1,0:T(2,128)(2,1)} %reshape.36), calls=%async_computation | async-start | bytes 98304 | tf_op jit(solution)/shard_map/all_to_all | solution.py:63
  156.8 24.7 %all-gather.4 = f32[16,1,512]{2,1,0:T(1,128)S(1)} all-gather(f32[1,1,512]{2,1,0:T(1,128)S(1)} %bitcast.49), channel_id=2, replica_groups=mesh['dp'=16,'cores'=8] {'dp'}, dimensions={0}, use_global_device_ids=true | all-gather | bytes 34816 | tf_op jit(solution)/shard_map/all_gather | solution.py:10
  181.4 19.4 %all-gather.5 = f32[16,1,512]{2,1,0:T(1,128)S(1)} all-gather(f32[1,1,512]{2,1,0:T(1,128)S(1)} %bitcast.48), channel_id=3, replica_groups=mesh['dp'=16,'cores'=8] {'dp'}, dimensions={0}, use_global_device_ids=true | all-gather | bytes 34816 | tf_op jit(solution)/shard_map/all_gather | solution.py:10
  200.9 0.0 all-to-all-done
  200.9 0.2 reshape.37
  201.1 0.1 copy.12
  201.2 92.6 %all-gather.11.cloned.1.call-done = f32[8192,768]{1,0:T(8,128)} async-done(((f32[512,768]{1,0:T(8,128)}), f32[8192,768]{1,0:T(8,128)}) %all-gather.11.cloned.1.call-update) | async-done | bytes 25165840 | tf_op jit(solution)/shard_map/all_gather | solution.py:10
  293.8 1.5 slice.19
  295.3 27.4 %while.19 = (s32[]{:T(128)}, f32[512]{0:T(512)S(1)}, f32[512]{0:T(512)S(1)}, f32[512,768]{1,0:T(8,128)S(1)}, f32[16,512]{1,0:T(8,128)S(1)}, /*index=5*/f32[16,51...) while((s32[]{:T(128)}, f32[512]{0:T(512)S(1)}, f32[512]{0:T(512)S(1)}, ...), condition=%wide.region_5.0_spmd, body=%wide.region_4.0_spmd.sunk | while | flops 1182725 | bytes 4747407 | solution.py:16
  295.4 1.8 fusion.15
  297.2 1.8 fusion.15
  299.0 1.8 fusion.15
  300.8 1.8 fusion.15
  302.7 1.8 fusion.15
  304.5 1.8 fusion.15
  306.3 1.8 fusion.15
  308.2 1.8 fusion.15
  310.0 1.8 fusion.15
  311.8 1.8 fusion.15
  313.6 1.8 fusion.15
  315.5 1.8 fusion.15
  317.3 1.8 fusion.15
  319.1 1.8 fusion.15
  321.0 1.8 fusion.15
  322.7 0.5 copy.11
  323.2 0.7 divide_subtract_fusion
  (39 shorter events, 0.6 us)
Async XLA Ops:
  6.5 135.3 %all-gather.9.cloned.1.call-start = ((), (), s32[]{:S(2)}) async-start(), calls=%async_computation.1 | async-start | bytes 7077888 | tf_op jit(solution)/shard_map/all_gather | solution.py:53
  7.3 286.5 %all-gather.11.cloned.1.call-start = ((), (), s32[]{:S(2)}) async-start(), calls=%async_computation.2 | async-start | bytes 26738688 | tf_op jit(solution)/shard_map/all_gather | solution.py:10
  14.0 2.8 copy-start.2
  16.8 4.6 %copy-start.1 = (bf16[512]{0:T(512)(128)(2,1)S(1)}, bf16[512]{0:T(512)(128)(2,1)}, u32[]{:S(2)}) copy-start(bf16[512]{0:T(512)(128)(2,1)} %param.9) | copy-start | bytes 3076
  141.9 5.3 %copy-start = (bf16[4096,768]{1,0:T(8,128)(2,1)S(1)}, bf16[4096,768]{1,0:T(8,128)(2,1)}, u32[]{:S(2)}) copy-start(bf16[4096,768]{1,0:T(8,128)(2,1)} %all-gather.9.cloned.1.call-done) | copy-start | bytes 18874372
  149.4 51.5 %all-to-all-start = ((bf16[16,2,768]{2,1,0:T(2,128)(2,1)}), bf16[16,2,768]{2,1,0:T(2,128)(2,1)S(1)}, u32[]{:S(2)}, u32[]{:S(2)}) async-start(bf16[16,2,768]{2,1,0:T(2,128)(2,1)} %reshape.36), calls=%async_computation | async-start | bytes 98304 | tf_op jit(solution)/shard_map/all_to_all | solution.py:63
Sparse Core Ops, SparseCore 0:
  9.0 132.8 all-gather.8
  144.3 149.3 all-gather.10
where the time goes:
time: 331 us
  waiting for transfers between devices  191 us (58%)
  blocking collectives  67.2 us (20%)
  other arithmetic  31 us (9%)
  matrix products  16.8 us (5%)
  between operations  13.5 us (4%)
  starting transfers between devices  7.39 us (2%)
  local copies, waits for them, and re-layouts  3.58 us (1%)
    all_gather x1, waiting for transfers between devices, on_device(): keys = lax.all_gather(coreset, 'cores', axis=0, tiled=True)  97.3 us
    all_gather x1, waiting for transfers between devices, joined(): everything = jax.tree.map(lambda part: lax.all_gather(part, axis), value)  92.6 us
    all_gather x2, blocking collectives, joined(): everything = jax.tree.map(lambda part: lax.all_gather(part, axis), value)  44.1 us
    add x15, other arithmetic, combine_parts(): first[2] * left[:, None] + second[2] * right[:, None]  26.4 us
    all_gather x1, blocking collectives, on_device(): potential = lax.all_gather(core_pot, 'cores', axis=0, tiled=True)  23.1 us
    all_to_all x1, starting transfers between devices, on_device(): lax.all_to_all(self_rows.astype(jnp.bfloat16), 'dp', split_axis=1, concat...  7.35 us
  transfers between devices with their start and end apart: 3, of which 2 were waited for; matrix products, arithmetic and copies ran while one was open for 7% of the time, Pallas kernels for 0%

commit v1 on v0

v1 whole, which is shorter than its diff:
```python
import functools
import math

import jax
import jax.numpy as jnp
from jax import lax
from jax.experimental import pallas as pl
from jax.experimental.pallas import tpu as pltpu
from jax.sharding import PartitionSpec as P

ROWS = 48
STATS = 8
TAIL = 16
VMEM_LIMIT = 48 * 2**20


def whole():
    return pl.BlockSpec(memory_space=pltpu.VMEM)


def fold(op, value):
    out = value[:, :128]
    for k in range(128, value.shape[1], 128):
        out = op(out, value[:, k : k + 128])
    return out


def write_halves(core, acc, top, total, send_ref, keep_ref, stat_ref):
    count, width = acc.shape
    lane = lax.broadcasted_iota(jnp.int32, (count, 128), 1)
    stats = jnp.where(lane == 0, top, total).T[:STATS]
    stat_ref[...] = stats
    half = width // 2
    send_ref[half:, :] = stats
    for j in range(0, width, 8 * ROWS):
        turned = acc[:, j : j + 8 * ROWS].T
        for i in range(4):
            first = turned[2 * ROWS * i : 2 * ROWS * i + ROWS]
            second = turned[2 * ROWS * i + ROWS : 2 * ROWS * (i + 1)]
            at = j // 2 + ROWS * i
            keep_ref[at : at + ROWS, :] = jnp.where(core == 0, first, second)
            send_ref[at : at + ROWS, :] = jnp.where(core == 0, second, first)


def cross_kernel(
    core_ref, pot_ref, query_ref, data_ref, send_ref, keep_ref, stat_ref,
    held, scores, weights, acc, top, total, sems,
):
    count, width = data_ref.shape
    cuts = (0, 512, 1024, count)
    step = 512
    part = width // 2
    scale = 30.0 / math.sqrt(width)
    copies = {
        a: pltpu.make_async_copy(data_ref.at[pl.ds(a, b - a)], held.at[pl.ds(a, b - a)], sems.at[i])
        for i, (a, b) in enumerate(zip(cuts, cuts[1:]))
    }
    for copy in copies.values():
        copy.start()
    for i in range(0, count, step):
        if i in copies:
            copies[i].wait()
        s = lax.dot_general(
            query_ref[...], held[i : i + step, :], (((1,), (1,)), ((), ())), preferred_element_type=jnp.float32
        )
        s = s * scale + pot_ref[:, i : i + step].astype(jnp.float32)
        scores[:, i : i + step] = s
        largest = fold(jnp.maximum, s)
        top[...] = largest if i == 0 else jnp.maximum(top[...], largest)
    top[...] = jnp.broadcast_to(jnp.max(top[...], axis=1, keepdims=True), top.shape)

    def soften(i, first, last):
        added = None
        for k in range(first, last, 128):
            p = jnp.exp(scores[:, i + k : i + k + 128] - top[...])
            weights[(i // step) % 2, :, k : k + 128] = p.astype(jnp.bfloat16)
            added = p if added is None else added + p
        total[...] = added if i + first == 0 else total[...] + added

    soften(0, 0, step)
    for i in range(0, count, step):
        for t in range(2):
            if i + step < count:
                soften(i + step, step // 2 * t, step // 2 * (t + 1))
            columns = slice(part * t, part * (t + 1))
            d = jnp.dot(weights[(i // step) % 2], held[i : i + step, columns], preferred_element_type=jnp.float32)
            acc[:, columns] = d if i == 0 else acc[:, columns] + d
    summed = jnp.sum(total[...], axis=1, keepdims=True)
    write_halves(core_ref[0], acc, top[...], summed, send_ref, keep_ref, stat_ref)


def self_kernel(core_ref, query_ref, key_ref, send_ref, keep_ref, stat_ref, acc):
    count, width = query_ref.shape
    number = key_ref.shape[0] - TAIL
    scale = 30.0 / math.sqrt(width)
    keys = key_ref[:number, :]
    pot = key_ref[number:, :number].astype(jnp.float32)[:1]
    s = scale * lax.dot_general(query_ref[...], keys, (((1,), (1,)), ((), ())), preferred_element_type=jnp.float32)
    s = s + pot
    top = jnp.max(s, axis=1, keepdims=True)
    p = jnp.exp(s - top)
    total = jnp.sum(p, axis=1, keepdims=True)
    acc[...] = jnp.dot(p.astype(jnp.bfloat16), keys, preferred_element_type=jnp.float32)
    top = jnp.broadcast_to(top, (count, 128))
    write_halves(core_ref[0], acc, top, total, send_ref, keep_ref, stat_ref)


def pair_kernel(keep_u, stat_u, come_u, keep_v, stat_v, come_v, out_ref):
    half = keep_u.shape[0]
    kept = []
    for n, (keep, stat, come) in enumerate(((keep_u, stat_u, come_u), (keep_v, stat_v, come_v))):
        other = come[half:, :]
        top = jnp.maximum(stat[0:1], other[0:1])
        left, right = jnp.exp(stat[0:1] - top), jnp.exp(other[0:1] - top)
        kept += [top, stat[1:2] * left + other[1:2] * right]
        for i in range(half // ROWS):
            rows = slice(ROWS * i, ROWS * (i + 1))
            out_ref[i, ROWS * n : ROWS * (n + 1), :] = (keep[rows] * left + come[rows] * right).astype(jnp.bfloat16)
    exact = jnp.concatenate(kept, 0)
    high = exact.astype(jnp.bfloat16).astype(jnp.float32)
    middle = (exact - high).astype(jnp.bfloat16).astype(jnp.float32)
    low = exact - high - middle
    tail = jnp.concatenate([high, middle, low, jnp.zeros_like(low)], 0).astype(jnp.bfloat16)
    for i in range(half // ROWS):
        out_ref[i, 2 * ROWS :, :] = tail


def last_kernel(come_ref, out_ref):
    chips = come_ref.shape[0]
    stats = []
    for i in range(chips):
        tail = come_ref[i, 2 * ROWS :, :].astype(jnp.float32)
        stats.append(tail[0:4] + tail[4:8] + tail[8:12])
    results = []
    for n in range(2):
        tops = [s[2 * n : 2 * n + 1] for s in stats]
        top = functools.reduce(jnp.maximum, tops)
        shares = [jnp.exp(t - top) for t in tops]
        total = sum(share * s[2 * n + 1 : 2 * n + 2] for share, s in zip(shares, stats))
        summed = sum(
            share * come_ref[i, ROWS * n : ROWS * (n + 1), :].astype(jnp.float32) for i, share in enumerate(shares)
        )
        results.append(summed / total)
    out_ref[...] = results[1] - results[0]


def on_device(data, data_pot, coreset, core_pot):
    count, width = coreset.shape
    half = width // 2
    chips = width // (2 * ROWS)
    position = lax.axis_index("dp")
    shards, blocks = lax.axis_size("dp"), lax.axis_size("cores")
    core = (position % 2).astype(jnp.int32).reshape(1)
    f32 = jnp.float32
    params = pltpu.CompilerParams(vmem_limit_bytes=VMEM_LIMIT)

    number = count * blocks // shards
    own = lax.dynamic_slice_in_dim(coreset, (position % 2) * number, number, 0)
    own_pot = lax.dynamic_slice_in_dim(core_pot, (position % 2) * number, number, 0)
    row = jnp.pad(own_pot[None, :], ((0, TAIL - 1), (0, width - number)))
    pairs = [(d * blocks + (c + d // 2) % blocks, d * blocks + c) for d in range(shards) for c in range(blocks)]
    keys = lax.ppermute(jnp.concatenate([own, row], 0), ("dp", "cores"), pairs)

    outs = [
        jax.ShapeDtypeStruct((half + STATS, count), f32),
        jax.ShapeDtypeStruct((half, count), f32),
        jax.ShapeDtypeStruct((STATS, count), f32),
    ]
    smem = pl.BlockSpec(memory_space=pltpu.SMEM)
    items = data.shape[0]
    send_u, keep_u, stat_u = pl.pallas_call(
        cross_kernel,
        out_shape=outs,
        in_specs=[smem, whole(), whole(), pl.BlockSpec(memory_space=pl.ANY)],
        out_specs=[whole()] * 3,
        scratch_shapes=[
            pltpu.VMEM((items, width), jnp.bfloat16),
            pltpu.VMEM((count, items), f32),
            pltpu.VMEM((2, count, 512), jnp.bfloat16),
            pltpu.VMEM((count, width), f32),
            pltpu.VMEM((count, 128), f32),
            pltpu.VMEM((count, 128), f32),
            pltpu.SemaphoreType.DMA((3,)),
        ],
        compiler_params=params,
        cost_estimate=pl.CostEstimate(
            flops=4 * count * items * width, bytes_accessed=2 * items * width, transcendentals=count * items
        ),
        name="cross",
    )(core, data_pot.reshape(1, items), coreset, data)
    swap = [(d, d ^ 1) for d in range(shards)]
    come_u = lax.ppermute(send_u, "dp", swap)
    send_v, keep_v, stat_v = pl.pallas_call(
        self_kernel,
        out_shape=outs,
        in_specs=[smem, whole(), whole()],
        out_specs=[whole()] * 3,
        scratch_shapes=[pltpu.VMEM((count, width), f32)],
        compiler_params=params,
        cost_estimate=pl.CostEstimate(
            flops=4 * count * number * width, bytes_accessed=4 * count * width, transcendentals=count * number
        ),
        name="self",
    )(core, coreset, keys)
    come_v = lax.ppermute(send_v, "dp", swap)
    merged = pl.pallas_call(
        pair_kernel,
        out_shape=jax.ShapeDtypeStruct((chips, 2 * ROWS + TAIL, count), jnp.bfloat16),
        in_specs=[whole()] * 6,
        out_specs=whole(),
        compiler_params=params,
        name="pair",
    )(keep_u, stat_u, come_u, keep_v, stat_v, come_v)
    groups = [[2 * i + k for i in range(chips)] for k in range(2)]
    come = lax.all_to_all(merged, "dp", 0, 0, axis_index_groups=groups, tiled=True)
    return pl.pallas_call(
        last_kernel,
        out_shape=jax.ShapeDtypeStruct((ROWS, count), f32),
        in_specs=[whole()],
        out_specs=whole(),
        compiler_params=params,
        name="last",
    )(come).T


def solution(mesh):
    return jax.shard_map(
        on_device,
        mesh=mesh,
        in_specs=(P("dp", None), P("dp"), P("cores", None), P("cores")),
        out_specs=P("cores", "dp"),
        check_vma=False,
    )
```

time: 331 us -> 48.2 us (0.15)
  waiting for transfers between devices: 191 us -> 2.28 us
  blocking collectives: 67.2 us -> 25 us
  other arithmetic: 31 us -> 0.03 us
  matrix products: 16.8 us -> 0 us
  Pallas kernels: 0 us -> 14.4 us
  between operations: 13.5 us -> 0.06 us
  starting transfers between devices: 7.39 us -> 2.3 us
    all_gather x2 -> x0, waiting for transfers between devices: 190 us -> none  [the longest x1 97.3 us: on_device(): keys = lax.all_gather(coreset, 'cores', axis=0, tiled=True)]
    all_gather x3 -> x0, blocking collectives: 67.2 us -> none  [the longest x2 44.1 us: joined(): everything = jax.tree.map(lambda part: lax.all_gather(part, axis), value)]
    add x30 -> x0, other arithmetic: 26.7 us -> none  [the longest x15 26.4 us: combine_parts(): first[2] * left[:, None] + second[2] * right[:, None]]
    all_to_all x0 -> x1, blocking collectives: none -> 25 us  [on_device(): lax.all_to_all(merged, 'dp', 0, 0, axis_index_groups=groups, tiled=True)]
    dot_general x4 -> x0, matrix products: 16.8 us -> none  [the longest x1 5.95 us: on_device(): lax.dot_general(coreset, data, (((1,), (1,)), ((), ())), preferred_elemen...]
    pallas_call x0 -> x4, Pallas kernels: none -> 14.4 us  [the longest x1 12 us: on_device(): pl.pallas_call(cross_kernel, out_shape=outs, in_specs=[smem, whole(), who...]
    all_to_all x1 -> x0, starting transfers between devices: 7.35 us -> none  [on_device(): lax.all_to_all(self_rows.astype(jnp.bfloat16), 'dp', split_axis=1, concat...]
  transfers between devices with their start and end apart: 3 -> 3, of which waited for: 2 -> 2; matrix products, arithmetic and copies ran while one was open for 7% -> 1% of each run, Pallas kernels for 0% -> 28%
where the time goes in v1:
time: 48.2 us; the launch traced here: 47.7 us
  blocking collectives  25 us (52%)
  Pallas kernels  14.4 us (30%)
  local copies, waits for them, and re-layouts  3.62 us (8%)
  starting transfers between devices  2.3 us (5%)
  waiting for transfers between devices  2.28 us (5%)
    all_to_all x1, blocking collectives, on_device(): lax.all_to_all(merged, 'dp', 0, 0, axis_index_groups=groups, tiled=True)  25 us
    pallas_call x1, Pallas kernels, on_device(): pl.pallas_call(cross_kernel, out_shape=outs, in_specs=[smem, whole(), who...  12 us
    ppermute x1, waiting for transfers between devices, on_device(): come_v = lax.ppermute(send_v, 'dp', swap)  1.74 us
    ppermute x1, starting transfers between devices, on_device(): come_u = lax.ppermute(send_u, 'dp', swap)  1.5 us
    pallas_call x1, Pallas kernels, on_device(): pl.pallas_call(self_kernel, out_shape=outs, in_specs=[smem, whole(), whol...  1.28 us
    unnamed x4, local copies, waits for them, and re-layouts  1.13 us
    dynamic_slice x1, local copies, waits for them, and re-layouts, on_device(): own = lax.dynamic_slice_in_dim(coreset, position % 2 * number, number, 0)  1.02 us
  transfers between devices with their start and end apart: 3, of which 2 were waited for; matrix products, arithmetic and copies ran while one was open for 1% of the time, Pallas kernels for 28%

profile of v1, /device:TPU:1, one launch (start us, length us, event | category | flops | bytes accessed | tf_op | source)
XLA Modules:
  0.0 47.7 jit_solution(7171104791529062250)
XLA Ops:
  0.0 0.8 %dynamic_slice.7 = bf16[256]{0:T(256)(128)(2,1)S(1)} dynamic-slice(bf16[512]{0:T(512)(128)(2,1)} %param.7, s32[]{:T(128)S(6)} %select_n.16), dynamic_slice_sizes={256} | dynamic-slice | bytes 1028 | tf_op jit(solution)/shard_map/dynamic_slice | solution.py:159
  0.8 1.0 %constant_dynamic-slice_fusion = bf16[256,768]{1,0:T(8,128)(2,1)S(1)} fusion(bf16[512,768]{1,0:T(8,128)(2,1)} %query_ref.3, s32[]{:T(128)S(6)} %select_n.16), kind=kLoop, calls=%fused_computation.3 | loop fusion | bytes 786436 | tf_op jit(solution)/shard_map/dynamic_slice | solution.py:158
  1.8 0.7 %collective-permute-start.1 = (bf16[272,768]{1,0:T(8,128)(2,1)S(1)}, bf16[272,768]{1,0:T(8,128)(2,1)S(1)}, u32[]{:S(2)}, u32[]{:S(2)}) collective-permute-start(bf16[272,768]{1,0:T(8,128)(2,1)S(1)} %fusion.1), channel_id=1, source_target_pairs={{0,0},{1,1},{2,2},{3,3},{4,4},{5,5},{6,6},{7,7},{8,8},{9,9},{10,10... | collective-permute-start | bytes 1253384 | tf_op jit(solution)/shard_map/ppermute | solution.py:162
  2.5 0.7 %reshape.7.pot_ref = bf16[1,4096]{1,0:T(2,128)(2,1)S(1)} reshape(bf16[4096]{0:T(1024)(128)(2,1)} %param.5) | data formatting | bytes 16384 | tf_op jit(solution)/shard_map/reshape | solution.py:190
  3.2 0.0 copy-start
  3.2 1.1 %copy-done = bf16[512,768]{1,0:T(8,128)(2,1)S(1)} copy-done((bf16[512,768]{1,0:T(8,128)(2,1)S(1)}, bf16[512,768]{1,0:T(8,128)(2,1)}, u32[]{:S(2)}) %copy-start) | copy-done | bytes 786456
  4.4 0.0 copy-start.1
  4.4 12.0 %cross.1 = (f32[392,512]{1,0:T(8,128)S(1)}, f32[384,512]{1,0:T(8,128)S(1)}, f32[8,512]{1,0:T(8,128)S(1)}) custom-call(s32[1]{0:T(128)} %bitcast.core_ref, bf16[1,4096]{1,0:T(2,128)(2,1)S(1)} %reshape.7.pot_ref, bf16[512,768]{1,0:T(8,128)(2,1)S(1)} %copy-done, bf16[4096,768]{1,0:T(8,128)(2,1)} %data_ref.1), custom_call_target="tpu_custom_call" | custom-call | flops 6442450944 | bytes 6291456 | tf_op jit(solution)/shard_map/cross/pallas_call | solution.py:171
  16.4 1.5 %collective-permute-start = (f32[392,512]{1,0:T(8,128)S(1)}, f32[392,512]{1,0:T(8,128)S(1)}, u32[]{:S(2)}, u32[]{:S(2)}) collective-permute-start(f32[392,512]{1,0:T(8,128)S(1)} %get-tuple-element.13), channel_id=1, source_target_pairs={{0,8},{8,0},{16,24},{24,16},{32,40},{40,32},{48,56},{56,48},{64,72... | collective-permute-start | bytes 2408456 | tf_op jit(solution)/shard_map/ppermute | solution.py:192
  17.9 0.0 collective-permute-done.1.key_ref
  17.9 0.0 copy-done.1
  17.9 1.3 %self.1 = (f32[392,512]{1,0:T(8,128)S(1)}, f32[384,512]{1,0:T(8,128)S(1)}, f32[8,512]{1,0:T(8,128)S(1)}) custom-call(s32[1]{0:T(128)} %bitcast.core_ref, bf16[512,768]{1,0:T(8,128)(2,1)S(1)} %copy-done.1, bf16[272,768]{1,0:T(8,128)(2,1)S(1)} %collective-permute-done.1.key_ref), custom_call_target="tpu_custom_call" | custom-call | flops 402653184 | bytes 1572864 | tf_op jit(solution)/shard_map/self/pallas_call | solution.py:193
  19.1 0.1 collective-permute-start.2
  19.3 0.5 %collective-permute-done.come_u = f32[392,512]{1,0:T(8,128)S(1)} collective-permute-done((f32[392,512]{1,0:T(8,128)S(1)}, f32[392,512]{1,0:T(8,128)S(1)}, u32[]{:S(2)}, u32[]{:S(2)}) %collective-permute-start) | collective-permute-done | bytes 802848 | tf_op jit(solution)/shard_map/ppermute | solution.py:192
  19.8 1.7 %collective-permute-done.2.come_v = f32[392,512]{1,0:T(8,128)S(1)} collective-permute-done((f32[392,512]{1,0:T(8,128)S(1)}, f32[392,512]{1,0:T(8,128)S(1)}, u32[]{:S(2)}, u32[]{:S(2)}) %collective-permute-start.2) | collective-permute-done | bytes 802848 | tf_op jit(solution)/shard_map/ppermute | solution.py:205
  21.5 0.2 pair.1
  21.8 25.0 %all_to_all.5.come_ref = bf16[8,112,512]{2,1,0:T(8,128)(2,1)S(1)} all-to-all(bf16[8,112,512]{2,1,0:T(8,128)(2,1)S(1)} %pair.1), channel_id=1, replica_groups={{0,16,32,48,64,80,96,112},{8,24,40,56,72,88,104,120},{1,17,33,49,65,81,..., dimensions={0} | all-to-all | bytes 1835008 | tf_op jit(solution)/shard_map/all_to_all | solution.py:215
  46.8 0.9 %last.1 = f32[48,512]{1,0:T(8,128)} custom-call(bf16[8,112,512]{2,1,0:T(8,128)(2,1)S(1)} %all_to_all.5.come_ref), custom_call_target="tpu_custom_call" | custom-call | tf_op jit(solution)/shard_map/last/pallas_call | solution.py:216
  (2 shorter events, 0.0 us)
Async XLA Ops:
  1.8 16.0 %collective-permute-start.1 = (bf16[272,768]{1,0:T(8,128)(2,1)S(1)}, bf16[272,768]{1,0:T(8,128)(2,1)S(1)}, u32[]{:S(2)}, u32[]{:S(2)}) collective-permute-start(bf16[272,768]{1,0:T(8,128)(2,1)S(1)} %fusion.1), channel_id=1, source_target_pairs={{0,0},{1,1},{2,2},{3,3},{4,4},{5,5},{6,6},{7,7},{8,8},{9,9},{10,10... | collective-permute-start | bytes 1253384 | tf_op jit(solution)/shard_map/ppermute | solution.py:162
  3.2 1.1 %copy-start = (bf16[512,768]{1,0:T(8,128)(2,1)S(1)}, bf16[512,768]{1,0:T(8,128)(2,1)}, u32[]{:S(2)}) copy-start(bf16[512,768]{1,0:T(8,128)(2,1)} %query_ref.3) | copy-start | bytes 2359300
  4.4 13.5 %copy-start.1 = (bf16[512,768]{1,0:T(8,128)(2,1)S(1)}, bf16[512,768]{1,0:T(8,128)(2,1)}, u32[]{:S(2)}) copy-start(bf16[512,768]{1,0:T(8,128)(2,1)} %query_ref.3) | copy-start | bytes 2359300
  16.4 3.4 %collective-permute-start = (f32[392,512]{1,0:T(8,128)S(1)}, f32[392,512]{1,0:T(8,128)S(1)}, u32[]{:S(2)}, u32[]{:S(2)}) collective-permute-start(f32[392,512]{1,0:T(8,128)S(1)} %get-tuple-element.13), channel_id=1, source_target_pairs={{0,8},{8,0},{16,24},{24,16},{32,40},{40,32},{48,56},{56,48},{64,72... | collective-permute-start | bytes 2408456 | tf_op jit(solution)/shard_map/ppermute | solution.py:192
  19.1 2.4 %collective-permute-start.2 = (f32[392,512]{1,0:T(8,128)S(1)}, f32[392,512]{1,0:T(8,128)S(1)}, u32[]{:S(2)}, u32[]{:S(2)}) collective-permute-start(f32[392,512]{1,0:T(8,128)S(1)} %get-tuple-element.16), channel_id=1, source_target_pairs={{0,8},{8,0},{16,24},{24,16},{32,40},{40,32},{48,56},{56,48},{64,72... | collective-permute-start | bytes 2408456 | tf_op jit(solution)/shard_map/ppermute | solution.py:205

commit v2 on v1

v2 whole, which is shorter than its diff:
```python
import functools
import math

import jax
import jax.numpy as jnp
from jax import lax
from jax.experimental import pallas as pl
from jax.experimental.pallas import tpu as pltpu
from jax.sharding import PartitionSpec as P

ROWS = 48
STATS = 8
TAIL = 16
REST = 8
WHENCE = (((0, 0), (2, 1)), ((0, 1), (2, 0)), ((1, 0), (3, 1)), ((1, 1), (3, 0)))
VMEM_LIMIT = 16 * 2**20


def whole():
    return pl.BlockSpec(memory_space=pltpu.VMEM)


def fold(op, value):
    out = value[:, :128]
    for k in range(128, value.shape[1], 128):
        out = op(out, value[:, k : k + 128])
    return out


def write_halves(core, acc, top, total, send_ref, keep_ref, stat_ref):
    count, width = acc.shape
    lane = lax.broadcasted_iota(jnp.int32, (count, 128), 1)
    stats = jnp.where(lane == 0, top, total).T[:STATS]
    stat_ref[...] = stats
    half = width // 2
    send_ref[half:, :] = stats
    for j in range(0, width, 8 * ROWS):
        turned = acc[:, j : j + 8 * ROWS].T
        for i in range(4):
            first = turned[2 * ROWS * i : 2 * ROWS * i + ROWS]
            second = turned[2 * ROWS * i + ROWS : 2 * ROWS * (i + 1)]
            at = j // 2 + ROWS * i
            keep_ref[at : at + ROWS, :] = jnp.where(core == 0, first, second)
            send_ref[at : at + ROWS, :] = jnp.where(core == 0, second, first)


def begin_kernel(core_ref, half_ref, out_ref):
    out_ref[...] = jnp.full(out_ref.shape, core_ref[0] + half_ref[0], out_ref.dtype)


def pack_kernel(after_ref, pot_ref, points_ref, key_ref):
    del after_ref
    number, width = points_ref.shape
    key_ref[:number, :] = points_ref[...]
    pot = pot_ref[...].astype(jnp.float32).reshape(1, number)
    row = jnp.concatenate([pot, jnp.zeros((1, width - number), jnp.float32)], 1)
    key_ref[number:, :] = jnp.broadcast_to(row, (TAIL, width)).astype(jnp.bfloat16)


def weigh_kernel(pot_ref, query_ref, data_ref, weights_ref, top_ref, total_ref, scores):
    count, width = data_ref.shape
    step = 512
    scale = 30.0 / math.sqrt(width)
    query = query_ref[: scores.shape[0], :]
    for i in range(0, count, step):
        s = lax.dot_general(
            query, data_ref[i : i + step, :], (((1,), (1,)), ((), ())), preferred_element_type=jnp.float32
        )
        s = s * scale + pot_ref[i : i + step].astype(jnp.float32).reshape(1, step)
        scores[:, i : i + step] = s
        largest = fold(jnp.maximum, s)
        top_ref[...] = largest if i == 0 else jnp.maximum(top_ref[...], largest)
    top_ref[...] = jnp.broadcast_to(jnp.max(top_ref[...], axis=1, keepdims=True), top_ref.shape)
    for i in range(0, count, step):
        added = None
        for k in range(i, i + step, 128):
            p = jnp.exp(scores[:, k : k + 128] - top_ref[...])
            weights_ref[:, k : k + 128] = p.astype(jnp.bfloat16)
            added = p if added is None else added + p
        total_ref[...] = added if i == 0 else total_ref[...] + added


def sum_kernel(core_ref, weights_ref, data_ref, top_ref, total_ref, send_ref, keep_ref, stat_ref, acc):
    acc[...] = jnp.dot(weights_ref[...], data_ref[...], preferred_element_type=jnp.float32)
    summed = jnp.sum(total_ref[...], axis=1, keepdims=True)
    write_halves(core_ref[0], acc, top_ref[...], summed, send_ref, keep_ref, stat_ref)


def self_kernel(core_ref, half_ref, query_ref, key_ref, after_ref, send_ref, keep_ref, stat_ref, acc):
    del after_ref
    count, width = acc.shape
    number = key_ref.shape[0] - TAIL
    scale = 30.0 / math.sqrt(width)
    query = query_ref[pl.ds(pl.multiple_of(half_ref[0] * count, count), count), :]
    keys = key_ref[:number, :]
    pot = key_ref[number:, :number].astype(jnp.float32)[:1]
    s = scale * lax.dot_general(query, keys, (((1,), (1,)), ((), ())), preferred_element_type=jnp.float32)
    s = s + pot
    top = jnp.max(s, axis=1, keepdims=True)
    p = jnp.exp(s - top)
    total = jnp.sum(p, axis=1, keepdims=True)
    acc[...] = jnp.dot(p.astype(jnp.bfloat16), keys, preferred_element_type=jnp.float32)
    top = jnp.broadcast_to(top, (count, 128))
    write_halves(core_ref[0], acc, top, total, send_ref, keep_ref, stat_ref)


def parted(value, number):
    pieces = []
    for _ in range(number):
        piece = value.astype(jnp.bfloat16).astype(jnp.float32)
        pieces.append(piece)
        value = value - piece
    return pieces


def pair_kernel(keep_u, stat_u, come_u, keep_v, stat_v, come_v, out_ref):
    half = keep_u.shape[0]
    merged = []
    for keep, stat, come in ((keep_u, stat_u, come_u), (keep_v, stat_v, come_v)):
        other = come[half:, :]
        top = jnp.maximum(stat[0:1], other[0:1])
        left, right = jnp.exp(stat[0:1] - top), jnp.exp(other[0:1] - top)
        merged.append((top, stat[1:2] * left + other[1:2] * right, left, right))
    (top_u, total_u, left_u, right_u), (top_v, total_v, left_v, right_v) = merged
    high, middle, low = parted(top_v, 3)
    main, rest = parted(total_v, 2)
    tail = parted(top_u, 3) + parted(total_u, 2)
    for pieces in ((high, middle), (low, main), (rest, jnp.zeros_like(rest))):
        tail.append(jnp.concatenate(pieces, 1))
    tail = jnp.concatenate(tail, 0)
    for i in range(half // ROWS):
        rows = slice(ROWS * i, ROWS * (i + 1))
        out_ref[i, :ROWS, :] = (keep_u[rows] * left_u + come_u[rows] * right_u).astype(jnp.bfloat16)
        v = keep_v[rows] * left_v + come_v[rows] * right_v
        v = jnp.concatenate([v[: ROWS // 2], v[ROWS // 2 :]], 1)
        out_ref[i, ROWS:, :] = jnp.concatenate([v, tail], 0).astype(jnp.bfloat16)


def joined(parts):
    top = functools.reduce(jnp.maximum, [t for t, _, _ in parts])
    shares = [jnp.exp(t - top) for t, _, _ in parts]
    total = sum(share * t for share, (_, t, _) in zip(shares, parts))
    return sum(share * value for share, (_, _, value) in zip(shares, parts)) / total


def last_kernel(come_ref, out_ref):
    chips = come_ref.shape[0]
    count = out_ref.shape[1] // 2
    cross, own = [], []
    for i in range(chips):
        u = come_ref[i, :ROWS, :].astype(jnp.float32)
        rest = come_ref[i, ROWS:, :].astype(jnp.float32)
        s = rest[ROWS // 2 :]
        cross.append((s[0:1] + s[1:2] + s[2:3], s[3:4] + s[4:5], u))
        top = s[5:6, :count] + s[5:6, count:] + s[6:7, :count]
        total = s[6:7, count:] + s[7:8, :count]
        own.append((jnp.concatenate([top, top], 1), jnp.concatenate([total, total], 1), rest[: ROWS // 2]))
    pull = joined(cross)
    for h in range(2):
        push = joined(own[h * chips // 2 : (h + 1) * chips // 2])
        lanes = slice(h * count, (h + 1) * count)
        out_ref[: ROWS // 2, lanes] = push[:, :count] - pull[: ROWS // 2, lanes]
        out_ref[ROWS // 2 :, lanes] = push[:, count:] - pull[ROWS // 2 :, lanes]


def on_device(data, data_pot, coreset, core_pot):
    count, width = coreset.shape
    items = data.shape[0]
    half = width // 2
    chips = width // (2 * ROWS)
    position = lax.axis_index("dp")
    shards, blocks = lax.axis_size("dp"), lax.axis_size("cores")
    core = (position % 2).astype(jnp.int32).reshape(1)
    x_hi = (position // chips).astype(jnp.int32).reshape(1)
    f32 = jnp.float32
    params = pltpu.CompilerParams(vmem_limit_bytes=VMEM_LIMIT)
    smem, anywhere = pl.BlockSpec(memory_space=pltpu.SMEM), pl.BlockSpec(memory_space=pl.ANY)

    begun = pl.pallas_call(
        begin_kernel,
        out_shape=jax.ShapeDtypeStruct((8, 128), jnp.int32),
        in_specs=[smem, smem],
        out_specs=whole(),
        compiler_params=params,
        cost_estimate=pl.CostEstimate(flops=10**11, bytes_accessed=4 * items * width, transcendentals=0),
        name="begin",
    )(core, x_hi)
    packed = pl.pallas_call(
        pack_kernel,
        out_shape=jax.ShapeDtypeStruct((count + TAIL, width), coreset.dtype),
        in_specs=[anywhere, whole(), whole()],
        out_specs=whole(),
        compiler_params=params,
        name="pack",
    )(begun, core_pot, coreset)
    pairs = []
    for d in range(shards):
        along, across = WHENCE[d // 2 % 4][d % 2]
        for c in range(blocks):
            source = (c // 2 + along) % 4 * 2 + (c % 2 ^ across)
            pairs.append((d * blocks + source, d * blocks + c))
    keys = lax.ppermute(packed, ("dp", "cores"), pairs)

    weights, top, total = pl.pallas_call(
        weigh_kernel,
        out_shape=[
            jax.ShapeDtypeStruct((count, items), jnp.bfloat16),
            jax.ShapeDtypeStruct((count, 128), f32),
            jax.ShapeDtypeStruct((count, 128), f32),
        ],
        in_specs=[whole()] * 3,
        out_specs=[whole()] * 3,
        scratch_shapes=[pltpu.VMEM((count, items), f32)],
        compiler_params=params,
        cost_estimate=pl.CostEstimate(
            flops=2 * count * items * width, bytes_accessed=2 * items * width, transcendentals=count * items
        ),
        name="weigh",
    )(data_pot, packed, data)

    def halves(number):
        return [
            jax.ShapeDtypeStruct((half + STATS, number), f32),
            jax.ShapeDtypeStruct((half, number), f32),
            jax.ShapeDtypeStruct((STATS, number), f32),
        ]

    swap = [(d, d ^ 1) for d in range(shards)]
    send_u, keep_u, stat_u = pl.pallas_call(
        sum_kernel,
        out_shape=halves(count),
        in_specs=[smem] + [whole()] * 4,
        out_specs=[whole()] * 3,
        scratch_shapes=[pltpu.VMEM((count, width), f32)],
        compiler_params=params,
        cost_estimate=pl.CostEstimate(
            flops=2 * count * items * width, bytes_accessed=2 * items * width, transcendentals=0
        ),
        name="sums",
    )(core, weights, data, top, total)
    come_u = lax.ppermute(send_u, "dp", swap)
    send_v, keep_v, stat_v = pl.pallas_call(
        self_kernel,
        out_shape=halves(count // 2),
        in_specs=[smem, smem, whole(), whole(), anywhere],
        out_specs=[whole()] * 3,
        scratch_shapes=[pltpu.VMEM((count // 2, width), f32)],
        compiler_params=params,
        cost_estimate=pl.CostEstimate(
            flops=2 * count * count * width, bytes_accessed=4 * count * width, transcendentals=count * count // 2
        ),
        name="self",
    )(core, x_hi, packed, keys, stat_u)
    come_v = lax.ppermute(send_v, "dp", swap)
    merged = pl.pallas_call(
        pair_kernel,
        out_shape=jax.ShapeDtypeStruct((chips, 3 * ROWS // 2 + REST, count), jnp.bfloat16),
        in_specs=[whole()] * 6,
        out_specs=whole(),
        compiler_params=params,
        name="pair",
    )(keep_u, stat_u, come_u, keep_v, stat_v, come_v)
    groups = [[2 * i + k for i in range(chips)] for k in range(2)]
    come = lax.all_to_all(merged, "dp", 0, 0, axis_index_groups=groups, tiled=True)
    return pl.pallas_call(
        last_kernel,
        out_shape=jax.ShapeDtypeStruct((ROWS, count), f32),
        in_specs=[whole()],
        out_specs=whole(),
        compiler_params=params,
        name="last",
    )(come).T


def solution(mesh):
    return jax.shard_map(
        on_device,
        mesh=mesh,
        in_specs=(P("dp", None), P("dp"), P("cores", None), P("cores")),
        out_specs=P("cores", "dp"),
        check_vma=False,
    )
```

time: 48.2 us -> 41.7 us (0.87)
  blocking collectives: 25 us -> 18.9 us
  starting transfers between devices: 2.3 us -> 7.7 us
  Pallas kernels: 14.4 us -> 10.6 us
  local copies, waits for them, and re-layouts: 3.62 us -> 1.11 us
    ppermute x1, starting transfers between devices: 0.69 us -> 7.52 us  [on_device(): keys = lax.ppermute(packed, ('dp', 'cores'), pairs)]
    all_to_all x1, blocking collectives: 25 us -> 18.9 us  [on_device(): lax.all_to_all(merged, 'dp', 0, 0, axis_index_groups=groups, tiled=True)]
    pallas_call x3 -> x6, Pallas kernels: 13.5 us -> 9.75 us  [the longest x1 4.82 us: on_device(): pl.pallas_call(weigh_kernel, out_shape=[jax.ShapeDtypeStruct((count, item...]
    dynamic_slice x2 -> x0, local copies, waits for them, and re-layouts: 1.77 us -> none  [the longest x1 1.02 us: on_device(): own = lax.dynamic_slice_in_dim(coreset, position % 2 * number, number, 0)]
    ppermute x1, starting transfers between devices: 1.5 us -> 0.09 us  [on_device(): come_u = lax.ppermute(send_u, 'dp', swap)]
    ppermute x1, waiting for transfers between devices: 0.01 us -> 1.01 us  [on_device(): keys = lax.ppermute(packed, ('dp', 'cores'), pairs)]
    reshape x1 -> x0, local copies, waits for them, and re-layouts: 0.71 us -> none  [on_device(): data_pot.reshape(1, items)]
    unnamed x4 -> x8, local copies, waits for them, and re-layouts: 1.13 us -> 1.11 us
  transfers between devices with their start and end apart: 3 -> 3, of which waited for: 2 -> 3; matrix products, arithmetic and copies ran while one was open for 1% -> 0% of each run, Pallas kernels for 28% -> 23%
where the time goes in v2:
time: 41.7 us; the launch traced here: 41.1 us
  blocking collectives  18.9 us (45%)
  Pallas kernels  10.6 us (25%)
  starting transfers between devices  7.7 us (18%)
  waiting for transfers between devices  2.73 us (7%)
  local copies, waits for them, and re-layouts  1.11 us (3%)
    all_to_all x1, blocking collectives, on_device(): lax.all_to_all(merged, 'dp', 0, 0, axis_index_groups=groups, tiled=True)  18.9 us
    ppermute x1, starting transfers between devices, on_device(): keys = lax.ppermute(packed, ('dp', 'cores'), pairs)  7.52 us
    pallas_call x1, Pallas kernels, on_device(): pl.pallas_call(weigh_kernel, out_shape=[jax.ShapeDtypeStruct((count, item...  4.82 us
    pallas_call x1, Pallas kernels, on_device(): pl.pallas_call(sum_kernel, out_shape=halves(count), in_specs=[smem] + [wh...  3.67 us
    ppermute x1, waiting for transfers between devices, on_device(): come_v = lax.ppermute(send_v, 'dp', swap)  1.53 us
    unnamed x8, local copies, waits for them, and re-layouts  1.11 us
    ppermute x1, waiting for transfers between devices, on_device(): keys = lax.ppermute(packed, ('dp', 'cores'), pairs)  1.01 us
    pallas_call x1, Pallas kernels, on_device(): pl.pallas_call(self_kernel, out_shape=halves(count // 2), in_specs=[smem,...  0.99 us
  transfers between devices with their start and end apart: 3, of which 3 were waited for; matrix products, arithmetic and copies ran while one was open for 0% of the time, Pallas kernels for 23%

profile of v2, /device:TPU:1, one launch (start us, length us, event | category | flops | bytes accessed | tf_op | source)
XLA Modules:
  0.0 41.1 jit_solution(626007720126967879)
XLA Ops:
  0.0 0.0 copy-start
  0.0 0.0 copy-start.1
  0.0 0.0 copy-start.2
  0.0 0.0 copy-start.3
  0.0 1.1 %copy-done = bf16[512,768]{1,0:T(8,128)(2,1)S(1)} copy-done((bf16[512,768]{1,0:T(8,128)(2,1)S(1)}, bf16[512,768]{1,0:T(8,128)(2,1)}, u32[]{:S(2)}) %copy-start) | copy-done | bytes 786456
  1.1 0.0 copy-done.1
  1.1 0.1 pack.1.query_ref
  1.2 7.5 %collective-permute-start.1 = (bf16[528,768]{1,0:T(8,128)(2,1)S(1)}, bf16[528,768]{1,0:T(8,128)(2,1)S(1)}, u32[]{:S(2)}, u32[]{:S(2)}) collective-permute-start(bf16[528,768]{1,0:T(8,128)(2,1)S(1)} %pack.1.query_ref), channel_id=1, source_target_pairs={{0,0},{1,1},{2,2},{3,3},{4,4},{5,5},{6,6},{7,7},{13,8},{12,9},{15,... | collective-permute-start | bytes 2433032 | tf_op jit(solution)/shard_map/ppermute | solution.py:202
  8.7 0.0 copy-done.2
  8.7 0.0 copy-done.3
  8.8 4.8 %weigh.1 = (bf16[512,4096]{1,0:T(8,128)(2,1)S(1)}, f32[512,128]{1,0:T(8,128)S(1)}, f32[512,128]{1,0:T(8,128)S(1)}) custom-call(bf16[4096]{0:T(1024)(128)(2,1)S(1)} %copy-done.3, bf16[528,768]{1,0:T(8,128)(2,1)S(1)} %pack.1.query_ref, bf16[4096,768]{1,0:T(8,128)(2,1)S(1)} %copy-done.2), custom_call_target="tpu_custom_call" | custom-call | flops 3221225472 | bytes 6291456 | tf_op jit(solution)/shard_map/weigh/pallas_call | solution.py:204
  13.6 3.7 %sums.1 = (f32[392,512]{1,0:T(8,128)S(1)}, f32[384,512]{1,0:T(8,128)S(1)}, f32[8,512]{1,0:T(8,128)S(1)}) custom-call(s32[1]{0:T(128)} %bitcast.core_ref, bf16[512,4096]{1,0:T(8,128)(2,1)S(1)} %get-tuple-element.14.weights_ref, bf16[4096,768]{1,0:T(8,128)(2,1)S(1)} %copy-done.2, f32[512,128]{1,0:T(8,128)S(1)} %get-tuple-element.15.top_ref, ...), custom_call_target="tpu_custom_call" | custom-call | flops 3221225472 | bytes 6291456 | tf_op jit(solution)/shard_map/sums/pallas_call | solution.py:229
  17.3 0.1 collective-permute-start
  17.4 1.0 %collective-permute-done.1.key_ref = bf16[528,768]{1,0:T(8,128)(2,1)S(1)} collective-permute-done((bf16[528,768]{1,0:T(8,128)(2,1)S(1)}, bf16[528,768]{1,0:T(8,128)(2,1)S(1)}, u32[]{:S(2)}, u32[]{:S(2)}) %collective-permute-start.1) | collective-permute-done | bytes 811040 | tf_op jit(solution)/shard_map/ppermute | solution.py:202
  18.4 1.0 %self.1 = (f32[392,256]{1,0:T(8,128)S(1)}, f32[384,256]{1,0:T(8,128)S(1)}, f32[8,256]{1,0:T(8,128)S(1)}) custom-call(s32[1]{0:T(128)} %bitcast.core_ref, s32[1]{0:T(128)} %bitcast.1.half_ref, bf16[528,768]{1,0:T(8,128)(2,1)S(1)} %pack.1.query_ref, bf16[528,768]{1,0:T(8,128)(2,1)S(1)} %collective-permute-done.1.key_ref, ...), custom_call_target="tpu_custom_call" | custom-call | flops 402653184 | bytes 1572864 | tf_op jit(solution)/shard_map/self/pallas_call | solution.py:242
  19.4 0.1 collective-permute-start.2
  19.5 0.2 collective-permute-done.come_u
  19.6 1.5 %collective-permute-done.2.come_v = f32[392,256]{1,0:T(8,128)S(1)} collective-permute-done((f32[392,256]{1,0:T(8,128)S(1)}, f32[392,256]{1,0:T(8,128)S(1)}, u32[]{:S(2)}, u32[]{:S(2)}) %collective-permute-start.2) | collective-permute-done | bytes 401440 | tf_op jit(solution)/shard_map/ppermute | solution.py:254
  21.2 0.2 pair.1
  21.4 18.9 %all_to_all.5.come_ref = bf16[8,80,512]{2,1,0:T(8,128)(2,1)S(1)} all-to-all(bf16[8,80,512]{2,1,0:T(8,128)(2,1)S(1)} %pair.1), channel_id=1, replica_groups={{0,16,32,48,64,80,96,112},{8,24,40,56,72,88,104,120},{1,17,33,49,65,81,..., dimensions={0} | all-to-all | bytes 1310720 | tf_op jit(solution)/shard_map/all_to_all | solution.py:264
  40.3 0.8 %last.1 = f32[48,512]{1,0:T(8,128)} custom-call(bf16[8,80,512]{2,1,0:T(8,128)(2,1)S(1)} %all_to_all.5.come_ref), custom_call_target="tpu_custom_call" | custom-call | tf_op jit(solution)/shard_map/last/pallas_call | solution.py:265
  (1 shorter events, 0.0 us)
Async XLA Ops:
  0.0 1.1 %copy-start = (bf16[512,768]{1,0:T(8,128)(2,1)S(1)}, bf16[512,768]{1,0:T(8,128)(2,1)}, u32[]{:S(2)}) copy-start(bf16[512,768]{1,0:T(8,128)(2,1)} %points_ref.1) | copy-start | bytes 2359300
  0.0 1.1 %copy-start.1 = (bf16[512]{0:T(512)(128)(2,1)S(1)}, bf16[512]{0:T(512)(128)(2,1)}, u32[]{:S(2)}) copy-start(bf16[512]{0:T(512)(128)(2,1)} %pot_ref.2) | copy-start | bytes 3076
  0.0 8.7 %copy-start.2 = (bf16[4096,768]{1,0:T(8,128)(2,1)S(1)}, bf16[4096,768]{1,0:T(8,128)(2,1)}, u32[]{:S(2)}) copy-start(bf16[4096,768]{1,0:T(8,128)(2,1)} %data_ref.3) | copy-start | bytes 18874372
  0.0 8.7 %copy-start.3 = (bf16[4096]{0:T(1024)(128)(2,1)S(1)}, bf16[4096]{0:T(1024)(128)(2,1)}, u32[]{:S(2)}) copy-start(bf16[4096]{0:T(1024)(128)(2,1)} %pot_ref.3) | copy-start | bytes 24580
  1.2 17.2 %collective-permute-start.1 = (bf16[528,768]{1,0:T(8,128)(2,1)S(1)}, bf16[528,768]{1,0:T(8,128)(2,1)S(1)}, u32[]{:S(2)}, u32[]{:S(2)}) collective-permute-start(bf16[528,768]{1,0:T(8,128)(2,1)S(1)} %pack.1.query_ref), channel_id=1, source_target_pairs={{0,0},{1,1},{2,2},{3,3},{4,4},{5,5},{6,6},{7,7},{13,8},{12,9},{15,... | collective-permute-start | bytes 2433032 | tf_op jit(solution)/shard_map/ppermute | solution.py:202
  17.3 2.4 %collective-permute-start = (f32[392,512]{1,0:T(8,128)S(1)}, f32[392,512]{1,0:T(8,128)S(1)}, u32[]{:S(2)}, u32[]{:S(2)}) collective-permute-start(f32[392,512]{1,0:T(8,128)S(1)} %get-tuple-element.19), channel_id=1, source_target_pairs={{0,8},{8,0},{16,24},{24,16},{32,40},{40,32},{48,56},{56,48},{64,72... | collective-permute-start | bytes 2408456 | tf_op jit(solution)/shard_map/ppermute | solution.py:241
  19.4 1.8 %collective-permute-start.2 = (f32[392,256]{1,0:T(8,128)S(1)}, f32[392,256]{1,0:T(8,128)S(1)}, u32[]{:S(2)}, u32[]{:S(2)}) collective-permute-start(f32[392,256]{1,0:T(8,128)S(1)} %get-tuple-element.22), channel_id=1, source_target_pairs={{0,8},{8,0},{16,24},{24,16},{32,40},{40,32},{48,56},{56,48},{64,72... | collective-permute-start | bytes 1204232 | tf_op jit(solution)/shard_map/ppermute | solution.py:254

commit v3 on v2

--- a/solution.py
+++ b/solution.py
@@ -12,7 +12,7 @@
 STATS = 8
 TAIL = 16
 REST = 8
-WHENCE = (((0, 0), (2, 1)), ((0, 1), (2, 0)), ((1, 0), (3, 1)), ((1, 1), (3, 0)))
+WHENCE = (((1, 1), (3, 0)), ((1, 0), (3, 1)), ((0, 1), (2, 0)), ((0, 0), (2, 1)))
 VMEM_LIMIT = 16 * 2**20
 
 

time: 41.7 us -> 40.9 us (0.981)
  starting transfers between devices: 7.7 us -> 9.95 us
  blocking collectives: 18.9 us -> 17.4 us
  waiting for transfers between devices: 2.73 us -> 1.36 us
    ppermute x1, starting transfers between devices: 0.09 us -> 4.09 us  [on_device(): come_u = lax.ppermute(send_u, 'dp', swap)]
    ppermute x1, starting transfers between devices: 7.52 us -> 4.64 us  [on_device(): keys = lax.ppermute(packed, ('dp', 'cores'), pairs)]
    all_to_all x1, blocking collectives: 18.9 us -> 17.4 us  [on_device(): lax.all_to_all(merged, 'dp', 0, 0, axis_index_groups=groups, tiled=True)]
    ppermute x1, starting transfers between devices: 0.09 us -> 1.22 us  [on_device(): come_v = lax.ppermute(send_v, 'dp', swap)]
    ppermute x1, waiting for transfers between devices: 1.01 us -> 0.01 us  [on_device(): keys = lax.ppermute(packed, ('dp', 'cores'), pairs)]
  transfers between devices with their start and end apart: 3 -> 3, of which waited for: 3 -> 1; matrix products, arithmetic and copies ran while one was open for 0% -> 0% of each run, Pallas kernels for 23% -> 23%
where the time goes in v3:
time: 40.9 us; the launch traced here: 40.5 us
  blocking collectives  17.4 us (43%)
  Pallas kernels  10.6 us (26%)
  starting transfers between devices  9.95 us (24%)
  waiting for transfers between devices  1.36 us (3%)
  local copies, waits for them, and re-layouts  1.11 us (3%)
    all_to_all x1, blocking collectives, on_device(): lax.all_to_all(merged, 'dp', 0, 0, axis_index_groups=groups, tiled=True)  17.4 us
    pallas_call x1, Pallas kernels, on_device(): pl.pallas_call(weigh_kernel, out_shape=[jax.ShapeDtypeStruct((count, item...  4.82 us
    ppermute x1, starting transfers between devices, on_device(): keys = lax.ppermute(packed, ('dp', 'cores'), pairs)  4.64 us
    ppermute x1, starting transfers between devices, on_device(): come_u = lax.ppermute(send_u, 'dp', swap)  4.09 us
    pallas_call x1, Pallas kernels, on_device(): pl.pallas_call(sum_kernel, out_shape=halves(count), in_specs=[smem] + [wh...  3.66 us
    ppermute x1, waiting for transfers between devices, on_device(): come_v = lax.ppermute(send_v, 'dp', swap)  1.36 us
    ppermute x1, starting transfers between devices, on_device(): come_v = lax.ppermute(send_v, 'dp', swap)  1.22 us
    unnamed x8, local copies, waits for them, and re-layouts  1.11 us
  transfers between devices with their start and end apart: 3, of which 1 were waited for; matrix products, arithmetic and copies ran while one was open for 0% of the time, Pallas kernels for 23%

profile of v3, /device:TPU:1, one launch (start us, length us, event | category | flops | bytes accessed | tf_op | source)
XLA Modules:
  0.0 40.5 jit_solution(12437045113498005759)
XLA Ops:
  0.0 0.0 copy-start
  0.0 0.0 copy-start.1
  0.0 0.0 copy-start.2
  0.0 0.0 copy-start.3
  0.0 1.1 %copy-done = bf16[512,768]{1,0:T(8,128)(2,1)S(1)} copy-done((bf16[512,768]{1,0:T(8,128)(2,1)S(1)}, bf16[512,768]{1,0:T(8,128)(2,1)}, u32[]{:S(2)}) %copy-start) | copy-done | bytes 786456
  1.1 0.0 copy-done.1
  1.1 0.1 pack.1.query_ref
  1.2 4.6 %collective-permute-start.1 = (bf16[528,768]{1,0:T(8,128)(2,1)S(1)}, bf16[528,768]{1,0:T(8,128)(2,1)S(1)}, u32[]{:S(2)}, u32[]{:S(2)}) collective-permute-start(bf16[528,768]{1,0:T(8,128)(2,1)S(1)} %pack.1.query_ref), channel_id=1, source_target_pairs={{3,0},{2,1},{5,2},{4,3},{7,4},{6,5},{1,6},{0,7},{14,8},{15,9},{8,1... | collective-permute-start | bytes 2433032 | tf_op jit(solution)/shard_map/ppermute | solution.py:202
  5.8 0.0 copy-done.2
  5.9 0.0 copy-done.3
  5.9 4.8 %weigh.1 = (bf16[512,4096]{1,0:T(8,128)(2,1)S(1)}, f32[512,128]{1,0:T(8,128)S(1)}, f32[512,128]{1,0:T(8,128)S(1)}) custom-call(bf16[4096]{0:T(1024)(128)(2,1)S(1)} %copy-done.3, bf16[528,768]{1,0:T(8,128)(2,1)S(1)} %pack.1.query_ref, bf16[4096,768]{1,0:T(8,128)(2,1)S(1)} %copy-done.2), custom_call_target="tpu_custom_call" | custom-call | flops 3221225472 | bytes 6291456 | tf_op jit(solution)/shard_map/weigh/pallas_call | solution.py:204
  10.7 3.7 %sums.1 = (f32[392,512]{1,0:T(8,128)S(1)}, f32[384,512]{1,0:T(8,128)S(1)}, f32[8,512]{1,0:T(8,128)S(1)}) custom-call(s32[1]{0:T(128)} %bitcast.core_ref, bf16[512,4096]{1,0:T(8,128)(2,1)S(1)} %get-tuple-element.14.weights_ref, bf16[4096,768]{1,0:T(8,128)(2,1)S(1)} %copy-done.2, f32[512,128]{1,0:T(8,128)S(1)} %get-tuple-element.15.top_ref, ...), custom_call_target="tpu_custom_call" | custom-call | flops 3221225472 | bytes 6291456 | tf_op jit(solution)/shard_map/sums/pallas_call | solution.py:229
  14.4 4.1 %collective-permute-start = (f32[392,512]{1,0:T(8,128)S(1)}, f32[392,512]{1,0:T(8,128)S(1)}, u32[]{:S(2)}, u32[]{:S(2)}) collective-permute-start(f32[392,512]{1,0:T(8,128)S(1)} %get-tuple-element.19), channel_id=1, source_target_pairs={{0,8},{8,0},{16,24},{24,16},{32,40},{40,32},{48,56},{56,48},{64,72... | collective-permute-start | bytes 2408456 | tf_op jit(solution)/shard_map/ppermute | solution.py:241
  18.5 0.0 collective-permute-done.1.key_ref
  18.5 1.0 %self.1 = (f32[392,256]{1,0:T(8,128)S(1)}, f32[384,256]{1,0:T(8,128)S(1)}, f32[8,256]{1,0:T(8,128)S(1)}) custom-call(s32[1]{0:T(128)} %bitcast.core_ref, s32[1]{0:T(128)} %bitcast.1.half_ref, bf16[528,768]{1,0:T(8,128)(2,1)S(1)} %pack.1.query_ref, bf16[528,768]{1,0:T(8,128)(2,1)S(1)} %collective-permute-done.1.key_ref, ...), custom_call_target="tpu_custom_call" | custom-call | flops 402653184 | bytes 1572864 | tf_op jit(solution)/shard_map/self/pallas_call | solution.py:242
  19.5 1.2 %collective-permute-start.2 = (f32[392,256]{1,0:T(8,128)S(1)}, f32[392,256]{1,0:T(8,128)S(1)}, u32[]{:S(2)}, u32[]{:S(2)}) collective-permute-start(f32[392,256]{1,0:T(8,128)S(1)} %get-tuple-element.22), channel_id=1, source_target_pairs={{0,8},{8,0},{16,24},{24,16},{32,40},{40,32},{48,56},{56,48},{64,72... | collective-permute-start | bytes 1204232 | tf_op jit(solution)/shard_map/ppermute | solution.py:254
  20.7 0.0 collective-permute-done.come_u
  20.7 1.4 %collective-permute-done.2.come_v = f32[392,256]{1,0:T(8,128)S(1)} collective-permute-done((f32[392,256]{1,0:T(8,128)S(1)}, f32[392,256]{1,0:T(8,128)S(1)}, u32[]{:S(2)}, u32[]{:S(2)}) %collective-permute-start.2) | collective-permute-done | bytes 401440 | tf_op jit(solution)/shard_map/ppermute | solution.py:254
  22.0 0.2 pair.1
  22.2 17.4 %all_to_all.5.come_ref = bf16[8,80,512]{2,1,0:T(8,128)(2,1)S(1)} all-to-all(bf16[8,80,512]{2,1,0:T(8,128)(2,1)S(1)} %pair.1), channel_id=1, replica_groups={{0,16,32,48,64,80,96,112},{8,24,40,56,72,88,104,120},{1,17,33,49,65,81,..., dimensions={0} | all-to-all | bytes 1310720 | tf_op jit(solution)/shard_map/all_to_all | solution.py:264
  39.7 0.8 %last.1 = f32[48,512]{1,0:T(8,128)} custom-call(bf16[8,80,512]{2,1,0:T(8,128)(2,1)S(1)} %all_to_all.5.come_ref), custom_call_target="tpu_custom_call" | custom-call | tf_op jit(solution)/shard_map/last/pallas_call | solution.py:265
  (1 shorter events, 0.0 us)
Async XLA Ops:
  0.0 1.1 %copy-start = (bf16[512,768]{1,0:T(8,128)(2,1)S(1)}, bf16[512,768]{1,0:T(8,128)(2,1)}, u32[]{:S(2)}) copy-start(bf16[512,768]{1,0:T(8,128)(2,1)} %points_ref.1) | copy-start | bytes 2359300
  0.0 1.1 %copy-start.1 = (bf16[512]{0:T(512)(128)(2,1)S(1)}, bf16[512]{0:T(512)(128)(2,1)}, u32[]{:S(2)}) copy-start(bf16[512]{0:T(512)(128)(2,1)} %pot_ref.2) | copy-start | bytes 3076
  0.0 5.8 %copy-start.2 = (bf16[4096,768]{1,0:T(8,128)(2,1)S(1)}, bf16[4096,768]{1,0:T(8,128)(2,1)}, u32[]{:S(2)}) copy-start(bf16[4096,768]{1,0:T(8,128)(2,1)} %data_ref.3) | copy-start | bytes 18874372
  0.0 5.8 %copy-start.3 = (bf16[4096]{0:T(1024)(128)(2,1)S(1)}, bf16[4096]{0:T(1024)(128)(2,1)}, u32[]{:S(2)}) copy-start(bf16[4096]{0:T(1024)(128)(2,1)} %pot_ref.3) | copy-start | bytes 24580
  1.2 17.3 %collective-permute-start.1 = (bf16[528,768]{1,0:T(8,128)(2,1)S(1)}, bf16[528,768]{1,0:T(8,128)(2,1)S(1)}, u32[]{:S(2)}, u32[]{:S(2)}) collective-permute-start(bf16[528,768]{1,0:T(8,128)(2,1)S(1)} %pack.1.query_ref), channel_id=1, source_target_pairs={{3,0},{2,1},{5,2},{4,3},{7,4},{6,5},{1,6},{0,7},{14,8},{15,9},{8,1... | collective-permute-start | bytes 2433032 | tf_op jit(solution)/shard_map/ppermute | solution.py:202
  14.4 6.3 %collective-permute-start = (f32[392,512]{1,0:T(8,128)S(1)}, f32[392,512]{1,0:T(8,128)S(1)}, u32[]{:S(2)}, u32[]{:S(2)}) collective-permute-start(f32[392,512]{1,0:T(8,128)S(1)} %get-tuple-element.19), channel_id=1, source_target_pairs={{0,8},{8,0},{16,24},{24,16},{32,40},{40,32},{48,56},{56,48},{64,72... | collective-permute-start | bytes 2408456 | tf_op jit(solution)/shard_map/ppermute | solution.py:241
  19.5 2.6 %collective-permute-start.2 = (f32[392,256]{1,0:T(8,128)S(1)}, f32[392,256]{1,0:T(8,128)S(1)}, u32[]{:S(2)}, u32[]{:S(2)}) collective-permute-start(f32[392,256]{1,0:T(8,128)S(1)} %get-tuple-element.22), channel_id=1, source_target_pairs={{0,8},{8,0},{16,24},{24,16},{32,40},{40,32},{48,56},{56,48},{64,72... | collective-permute-start | bytes 1204232 | tf_op jit(solution)/shard_map/ppermute | solution.py:254

commit v4 on v3

--- a/solution.py
+++ b/solution.py
@@ -14,6 +14,8 @@
 REST = 8
 WHENCE = (((1, 1), (3, 0)), ((1, 0), (3, 1)), ((0, 1), (2, 0)), ((0, 0), (2, 1)))
 VMEM_LIMIT = 16 * 2**20
+
+ORDER = (4, 5, 6, 7, 0, 1, 2, 3)
 
 
 def whole():
@@ -130,10 +132,11 @@
     tail = jnp.concatenate(tail, 0)
     for i in range(half // ROWS):
         rows = slice(ROWS * i, ROWS * (i + 1))
-        out_ref[i, :ROWS, :] = (keep_u[rows] * left_u + come_u[rows] * right_u).astype(jnp.bfloat16)
+        to = ORDER.index(i)
+        out_ref[to, :ROWS, :] = (keep_u[rows] * left_u + come_u[rows] * right_u).astype(jnp.bfloat16)
         v = keep_v[rows] * left_v + come_v[rows] * right_v
         v = jnp.concatenate([v[: ROWS // 2], v[ROWS // 2 :]], 1)
-        out_ref[i, ROWS:, :] = jnp.concatenate([v, tail], 0).astype(jnp.bfloat16)
+        out_ref[to, ROWS:, :] = jnp.concatenate([v, tail], 0).astype(jnp.bfloat16)
 
 
 def joined(parts):
@@ -157,7 +160,7 @@
         own.append((jnp.concatenate([top, top], 1), jnp.concatenate([total, total], 1), rest[: ROWS // 2]))
     pull = joined(cross)
     for h in range(2):
-        push = joined(own[h * chips // 2 : (h + 1) * chips // 2])
+        push = joined([part for part, chip in zip(own, ORDER) if 2 * chip // chips == h])
         lanes = slice(h * count, (h + 1) * count)
         out_ref[: ROWS // 2, lanes] = push[:, :count] - pull[: ROWS // 2, lanes]
         out_ref[ROWS // 2 :, lanes] = push[:, count:] - pull[ROWS // 2 :, lanes]
@@ -260,7 +263,7 @@
         compiler_params=params,
         name="pair",
     )(keep_u, stat_u, come_u, keep_v, stat_v, come_v)
-    groups = [[2 * i + k for i in range(chips)] for k in range(2)]
+    groups = [[2 * i + k for i in ORDER] for k in range(2)]
     come = lax.all_to_all(merged, "dp", 0, 0, axis_index_groups=groups, tiled=True)
     return pl.pallas_call(
         last_kernel,

time: 40.9 us -> 38.9 us (0.951)
  blocking collectives: 17.4 us -> 15.7 us
    all_to_all x1, blocking collectives: 17.4 us -> 15.7 us  [on_device(): lax.all_to_all(merged, 'dp', 0, 0, axis_index_groups=groups, tiled=True)]
  transfers between devices with their start and end apart: 3 -> 3, of which waited for: 1 -> 1; matrix products, arithmetic and copies ran while one was open for 0% -> 0% of each run, Pallas kernels for 23% -> 24%
where the time goes in v4:
time: 38.9 us; the launch traced here: 38.7 us
  blocking collectives  15.7 us (40%)
  Pallas kernels  10.6 us (27%)
  starting transfers between devices  9.95 us (26%)
  waiting for transfers between devices  1.36 us (3%)
  local copies, waits for them, and re-layouts  1.11 us (3%)
    all_to_all x1, blocking collectives, on_device(): lax.all_to_all(merged, 'dp', 0, 0, axis_index_groups=groups, tiled=True)  15.7 us
    pallas_call x1, Pallas kernels, on_device(): pl.pallas_call(weigh_kernel, out_shape=[jax.ShapeDtypeStruct((count, item...  4.82 us
    ppermute x1, starting transfers between devices, on_device(): keys = lax.ppermute(packed, ('dp', 'cores'), pairs)  4.64 us
    ppermute x1, starting transfers between devices, on_device(): come_u = lax.ppermute(send_u, 'dp', swap)  4.09 us
    pallas_call x1, Pallas kernels, on_device(): pl.pallas_call(sum_kernel, out_shape=halves(count), in_specs=[smem] + [wh...  3.66 us
    ppermute x1, waiting for transfers between devices, on_device(): come_v = lax.ppermute(send_v, 'dp', swap)  1.36 us
    ppermute x1, starting transfers between devices, on_device(): come_v = lax.ppermute(send_v, 'dp', swap)  1.22 us
    unnamed x8, local copies, waits for them, and re-layouts  1.11 us
  transfers between devices with their start and end apart: 3, of which 1 were waited for; matrix products, arithmetic and copies ran while one was open for 0% of the time, Pallas kernels for 24%

profile of v4, /device:TPU:1, one launch (start us, length us, event | category | flops | bytes accessed | tf_op | source)
XLA Modules:
  0.0 38.7 jit_solution(9690713414853870290)
XLA Ops:
  0.0 0.0 copy-start
  0.0 0.0 copy-start.1
  0.0 0.0 copy-start.2
  0.0 0.0 copy-start.3
  0.0 1.1 %copy-done = bf16[512,768]{1,0:T(8,128)(2,1)S(1)} copy-done((bf16[512,768]{1,0:T(8,128)(2,1)S(1)}, bf16[512,768]{1,0:T(8,128)(2,1)}, u32[]{:S(2)}) %copy-start) | copy-done | bytes 786456
  1.1 0.0 copy-done.1
  1.1 0.1 pack.1.query_ref
  1.2 4.6 %collective-permute-start.1 = (bf16[528,768]{1,0:T(8,128)(2,1)S(1)}, bf16[528,768]{1,0:T(8,128)(2,1)S(1)}, u32[]{:S(2)}, u32[]{:S(2)}) collective-permute-start(bf16[528,768]{1,0:T(8,128)(2,1)S(1)} %pack.1.query_ref), channel_id=1, source_target_pairs={{3,0},{2,1},{5,2},{4,3},{7,4},{6,5},{1,6},{0,7},{14,8},{15,9},{8,1... | collective-permute-start | bytes 2433032 | tf_op jit(solution)/shard_map/ppermute | solution.py:205
  5.8 0.0 copy-done.2
  5.9 0.0 copy-done.3
  5.9 4.8 %weigh.1 = (bf16[512,4096]{1,0:T(8,128)(2,1)S(1)}, f32[512,128]{1,0:T(8,128)S(1)}, f32[512,128]{1,0:T(8,128)S(1)}) custom-call(bf16[4096]{0:T(1024)(128)(2,1)S(1)} %copy-done.3, bf16[528,768]{1,0:T(8,128)(2,1)S(1)} %pack.1.query_ref, bf16[4096,768]{1,0:T(8,128)(2,1)S(1)} %copy-done.2), custom_call_target="tpu_custom_call" | custom-call | flops 3221225472 | bytes 6291456 | tf_op jit(solution)/shard_map/weigh/pallas_call | solution.py:207
  10.7 3.7 %sums.1 = (f32[392,512]{1,0:T(8,128)S(1)}, f32[384,512]{1,0:T(8,128)S(1)}, f32[8,512]{1,0:T(8,128)S(1)}) custom-call(s32[1]{0:T(128)} %bitcast.core_ref, bf16[512,4096]{1,0:T(8,128)(2,1)S(1)} %get-tuple-element.14.weights_ref, bf16[4096,768]{1,0:T(8,128)(2,1)S(1)} %copy-done.2, f32[512,128]{1,0:T(8,128)S(1)} %get-tuple-element.15.top_ref, ...), custom_call_target="tpu_custom_call" | custom-call | flops 3221225472 | bytes 6291456 | tf_op jit(solution)/shard_map/sums/pallas_call | solution.py:232
  14.4 4.1 %collective-permute-start = (f32[392,512]{1,0:T(8,128)S(1)}, f32[392,512]{1,0:T(8,128)S(1)}, u32[]{:S(2)}, u32[]{:S(2)}) collective-permute-start(f32[392,512]{1,0:T(8,128)S(1)} %get-tuple-element.19), channel_id=1, source_target_pairs={{0,8},{8,0},{16,24},{24,16},{32,40},{40,32},{48,56},{56,48},{64,72... | collective-permute-start | bytes 2408456 | tf_op jit(solution)/shard_map/ppermute | solution.py:244
  18.5 0.0 collective-permute-done.1.key_ref
  18.5 1.0 %self.1 = (f32[392,256]{1,0:T(8,128)S(1)}, f32[384,256]{1,0:T(8,128)S(1)}, f32[8,256]{1,0:T(8,128)S(1)}) custom-call(s32[1]{0:T(128)} %bitcast.core_ref, s32[1]{0:T(128)} %bitcast.1.half_ref, bf16[528,768]{1,0:T(8,128)(2,1)S(1)} %pack.1.query_ref, bf16[528,768]{1,0:T(8,128)(2,1)S(1)} %collective-permute-done.1.key_ref, ...), custom_call_target="tpu_custom_call" | custom-call | flops 402653184 | bytes 1572864 | tf_op jit(solution)/shard_map/self/pallas_call | solution.py:245
  19.5 1.2 %collective-permute-start.2 = (f32[392,256]{1,0:T(8,128)S(1)}, f32[392,256]{1,0:T(8,128)S(1)}, u32[]{:S(2)}, u32[]{:S(2)}) collective-permute-start(f32[392,256]{1,0:T(8,128)S(1)} %get-tuple-element.22), channel_id=1, source_target_pairs={{0,8},{8,0},{16,24},{24,16},{32,40},{40,32},{48,56},{56,48},{64,72... | collective-permute-start | bytes 1204232 | tf_op jit(solution)/shard_map/ppermute | solution.py:257
  20.7 0.0 collective-permute-done.come_u
  20.7 1.4 %collective-permute-done.2.come_v = f32[392,256]{1,0:T(8,128)S(1)} collective-permute-done((f32[392,256]{1,0:T(8,128)S(1)}, f32[392,256]{1,0:T(8,128)S(1)}, u32[]{:S(2)}, u32[]{:S(2)}) %collective-permute-start.2) | collective-permute-done | bytes 401440 | tf_op jit(solution)/shard_map/ppermute | solution.py:257
  22.0 0.2 pair.1
  22.2 15.7 %all_to_all.5.come_ref = bf16[8,80,512]{2,1,0:T(8,128)(2,1)S(1)} all-to-all(bf16[8,80,512]{2,1,0:T(8,128)(2,1)S(1)} %pair.1), channel_id=1, replica_groups={{64,80,96,112,0,16,32,48},{72,88,104,120,8,24,40,56},{65,81,97,113,1,17..., dimensions={0} | all-to-all | bytes 1310720 | tf_op jit(solution)/shard_map/all_to_all | solution.py:267
  37.9 0.8 %last.1 = f32[48,512]{1,0:T(8,128)} custom-call(bf16[8,80,512]{2,1,0:T(8,128)(2,1)S(1)} %all_to_all.5.come_ref), custom_call_target="tpu_custom_call" | custom-call | tf_op jit(solution)/shard_map/last/pallas_call | solution.py:268
  (1 shorter events, 0.0 us)
Async XLA Ops:
  0.0 1.1 %copy-start = (bf16[512,768]{1,0:T(8,128)(2,1)S(1)}, bf16[512,768]{1,0:T(8,128)(2,1)}, u32[]{:S(2)}) copy-start(bf16[512,768]{1,0:T(8,128)(2,1)} %points_ref.1) | copy-start | bytes 2359300
  0.0 1.1 %copy-start.1 = (bf16[512]{0:T(512)(128)(2,1)S(1)}, bf16[512]{0:T(512)(128)(2,1)}, u32[]{:S(2)}) copy-start(bf16[512]{0:T(512)(128)(2,1)} %pot_ref.2) | copy-start | bytes 3076
  0.0 5.8 %copy-start.2 = (bf16[4096,768]{1,0:T(8,128)(2,1)S(1)}, bf16[4096,768]{1,0:T(8,128)(2,1)}, u32[]{:S(2)}) copy-start(bf16[4096,768]{1,0:T(8,128)(2,1)} %data_ref.3) | copy-start | bytes 18874372
  0.0 5.8 %copy-start.3 = (bf16[4096]{0:T(1024)(128)(2,1)S(1)}, bf16[4096]{0:T(1024)(128)(2,1)}, u32[]{:S(2)}) copy-start(bf16[4096]{0:T(1024)(128)(2,1)} %pot_ref.3) | copy-start | bytes 24580
  1.2 17.3 %collective-permute-start.1 = (bf16[528,768]{1,0:T(8,128)(2,1)S(1)}, bf16[528,768]{1,0:T(8,128)(2,1)S(1)}, u32[]{:S(2)}, u32[]{:S(2)}) collective-permute-start(bf16[528,768]{1,0:T(8,128)(2,1)S(1)} %pack.1.query_ref), channel_id=1, source_target_pairs={{3,0},{2,1},{5,2},{4,3},{7,4},{6,5},{1,6},{0,7},{14,8},{15,9},{8,1... | collective-permute-start | bytes 2433032 | tf_op jit(solution)/shard_map/ppermute | solution.py:205
  14.4 6.3 %collective-permute-start = (f32[392,512]{1,0:T(8,128)S(1)}, f32[392,512]{1,0:T(8,128)S(1)}, u32[]{:S(2)}, u32[]{:S(2)}) collective-permute-start(f32[392,512]{1,0:T(8,128)S(1)} %get-tuple-element.19), channel_id=1, source_target_pairs={{0,8},{8,0},{16,24},{24,16},{32,40},{40,32},{48,56},{56,48},{64,72... | collective-permute-start | bytes 2408456 | tf_op jit(solution)/shard_map/ppermute | solution.py:244
  19.5 2.6 %collective-permute-start.2 = (f32[392,256]{1,0:T(8,128)S(1)}, f32[392,256]{1,0:T(8,128)S(1)}, u32[]{:S(2)}, u32[]{:S(2)}) collective-permute-start(f32[392,256]{1,0:T(8,128)S(1)} %get-tuple-element.22), channel_id=1, source_target_pairs={{0,8},{8,0},{16,24},{24,16},{32,40},{40,32},{48,56},{56,48},{64,72... | collective-permute-start | bytes 1204232 | tf_op jit(solution)/shard_map/ppermute | solution.py:257

commit v5 on v4

--- a/solution.py
+++ b/solution.py
@@ -15,7 +15,7 @@
 WHENCE = (((1, 1), (3, 0)), ((1, 0), (3, 1)), ((0, 1), (2, 0)), ((0, 0), (2, 1)))
 VMEM_LIMIT = 16 * 2**20
 
-ORDER = (4, 5, 6, 7, 0, 1, 2, 3)
+ORDER = (6, 5, 4, 7, 2, 1, 0, 3)
 
 
 def whole():

time: 38.9 us -> 37.8 us (0.972)
  blocking collectives: 15.7 us -> 14.4 us
    all_to_all x1, blocking collectives: 15.7 us -> 14.4 us  [on_device(): lax.all_to_all(merged, 'dp', 0, 0, axis_index_groups=groups, tiled=True)]
  transfers between devices with their start and end apart: 3 -> 3, of which waited for: 1 -> 1; matrix products, arithmetic and copies ran while one was open for 0% -> 0% of each run, Pallas kernels for 24% -> 25%
where the time goes in v5:
time: 37.8 us; the launch traced here: 37.5 us
  blocking collectives  14.4 us (38%)
  Pallas kernels  10.6 us (28%)
  starting transfers between devices  9.95 us (26%)
  waiting for transfers between devices  1.36 us (4%)
  local copies, waits for them, and re-layouts  1.11 us (3%)
    all_to_all x1, blocking collectives, on_device(): lax.all_to_all(merged, 'dp', 0, 0, axis_index_groups=groups, tiled=True)  14.4 us
    pallas_call x1, Pallas kernels, on_device(): pl.pallas_call(weigh_kernel, out_shape=[jax.ShapeDtypeStruct((count, item...  4.82 us
    ppermute x1, starting transfers between devices, on_device(): keys = lax.ppermute(packed, ('dp', 'cores'), pairs)  4.64 us
    ppermute x1, starting transfers between devices, on_device(): come_u = lax.ppermute(send_u, 'dp', swap)  4.09 us
    pallas_call x1, Pallas kernels, on_device(): pl.pallas_call(sum_kernel, out_shape=halves(count), in_specs=[smem] + [wh...  3.66 us
    ppermute x1, waiting for transfers between devices, on_device(): come_v = lax.ppermute(send_v, 'dp', swap)  1.36 us
    ppermute x1, starting transfers between devices, on_device(): come_v = lax.ppermute(send_v, 'dp', swap)  1.22 us
    unnamed x8, local copies, waits for them, and re-layouts  1.11 us
  transfers between devices with their start and end apart: 3, of which 1 were waited for; matrix products, arithmetic and copies ran while one was open for 0% of the time, Pallas kernels for 25%

profile of v5, /device:TPU:1, one launch (start us, length us, event | category | flops | bytes accessed | tf_op | source)
XLA Modules:
  0.0 37.5 jit_solution(9291084173729793639)
XLA Ops:
  0.0 0.0 copy-start
  0.0 0.0 copy-start.1
  0.0 0.0 copy-start.2
  0.0 0.0 copy-start.3
  0.0 1.1 %copy-done = bf16[512,768]{1,0:T(8,128)(2,1)S(1)} copy-done((bf16[512,768]{1,0:T(8,128)(2,1)S(1)}, bf16[512,768]{1,0:T(8,128)(2,1)}, u32[]{:S(2)}) %copy-start) | copy-done | bytes 786456
  1.1 0.0 copy-done.1
  1.1 0.1 pack.1.query_ref
  1.2 4.6 %collective-permute-start.1 = (bf16[528,768]{1,0:T(8,128)(2,1)S(1)}, bf16[528,768]{1,0:T(8,128)(2,1)S(1)}, u32[]{:S(2)}, u32[]{:S(2)}) collective-permute-start(bf16[528,768]{1,0:T(8,128)(2,1)S(1)} %pack.1.query_ref), channel_id=1, source_target_pairs={{3,0},{2,1},{5,2},{4,3},{7,4},{6,5},{1,6},{0,7},{14,8},{15,9},{8,1... | collective-permute-start | bytes 2433032 | tf_op jit(solution)/shard_map/ppermute | solution.py:205
  5.8 0.0 copy-done.2
  5.9 0.0 copy-done.3
  5.9 4.8 %weigh.1 = (bf16[512,4096]{1,0:T(8,128)(2,1)S(1)}, f32[512,128]{1,0:T(8,128)S(1)}, f32[512,128]{1,0:T(8,128)S(1)}) custom-call(bf16[4096]{0:T(1024)(128)(2,1)S(1)} %copy-done.3, bf16[528,768]{1,0:T(8,128)(2,1)S(1)} %pack.1.query_ref, bf16[4096,768]{1,0:T(8,128)(2,1)S(1)} %copy-done.2), custom_call_target="tpu_custom_call" | custom-call | flops 3221225472 | bytes 6291456 | tf_op jit(solution)/shard_map/weigh/pallas_call | solution.py:207
  10.7 3.7 %sums.1 = (f32[392,512]{1,0:T(8,128)S(1)}, f32[384,512]{1,0:T(8,128)S(1)}, f32[8,512]{1,0:T(8,128)S(1)}) custom-call(s32[1]{0:T(128)} %bitcast.core_ref, bf16[512,4096]{1,0:T(8,128)(2,1)S(1)} %get-tuple-element.14.weights_ref, bf16[4096,768]{1,0:T(8,128)(2,1)S(1)} %copy-done.2, f32[512,128]{1,0:T(8,128)S(1)} %get-tuple-element.15.top_ref, ...), custom_call_target="tpu_custom_call" | custom-call | flops 3221225472 | bytes 6291456 | tf_op jit(solution)/shard_map/sums/pallas_call | solution.py:232
  14.4 4.1 %collective-permute-start = (f32[392,512]{1,0:T(8,128)S(1)}, f32[392,512]{1,0:T(8,128)S(1)}, u32[]{:S(2)}, u32[]{:S(2)}) collective-permute-start(f32[392,512]{1,0:T(8,128)S(1)} %get-tuple-element.19), channel_id=1, source_target_pairs={{0,8},{8,0},{16,24},{24,16},{32,40},{40,32},{48,56},{56,48},{64,72... | collective-permute-start | bytes 2408456 | tf_op jit(solution)/shard_map/ppermute | solution.py:244
  18.5 0.0 collective-permute-done.1.key_ref
  18.5 1.0 %self.1 = (f32[392,256]{1,0:T(8,128)S(1)}, f32[384,256]{1,0:T(8,128)S(1)}, f32[8,256]{1,0:T(8,128)S(1)}) custom-call(s32[1]{0:T(128)} %bitcast.core_ref, s32[1]{0:T(128)} %bitcast.1.half_ref, bf16[528,768]{1,0:T(8,128)(2,1)S(1)} %pack.1.query_ref, bf16[528,768]{1,0:T(8,128)(2,1)S(1)} %collective-permute-done.1.key_ref, ...), custom_call_target="tpu_custom_call" | custom-call | flops 402653184 | bytes 1572864 | tf_op jit(solution)/shard_map/self/pallas_call | solution.py:245
  19.5 1.2 %collective-permute-start.2 = (f32[392,256]{1,0:T(8,128)S(1)}, f32[392,256]{1,0:T(8,128)S(1)}, u32[]{:S(2)}, u32[]{:S(2)}) collective-permute-start(f32[392,256]{1,0:T(8,128)S(1)} %get-tuple-element.22), channel_id=1, source_target_pairs={{0,8},{8,0},{16,24},{24,16},{32,40},{40,32},{48,56},{56,48},{64,72... | collective-permute-start | bytes 1204232 | tf_op jit(solution)/shard_map/ppermute | solution.py:257
  20.7 0.0 collective-permute-done.come_u
  20.7 1.4 %collective-permute-done.2.come_v = f32[392,256]{1,0:T(8,128)S(1)} collective-permute-done((f32[392,256]{1,0:T(8,128)S(1)}, f32[392,256]{1,0:T(8,128)S(1)}, u32[]{:S(2)}, u32[]{:S(2)}) %collective-permute-start.2) | collective-permute-done | bytes 401440 | tf_op jit(solution)/shard_map/ppermute | solution.py:257
  22.0 0.2 pair.1
  22.2 14.4 %all_to_all.5.come_ref = bf16[8,80,512]{2,1,0:T(8,128)(2,1)S(1)} all-to-all(bf16[8,80,512]{2,1,0:T(8,128)(2,1)S(1)} %pair.1), channel_id=1, replica_groups={{96,80,64,112,32,16,0,48},{104,88,72,120,40,24,8,56},{97,81,65,113,33,1..., dimensions={0} | all-to-all | bytes 1310720 | tf_op jit(solution)/shard_map/all_to_all | solution.py:267
  36.7 0.8 %last.1 = f32[48,512]{1,0:T(8,128)} custom-call(bf16[8,80,512]{2,1,0:T(8,128)(2,1)S(1)} %all_to_all.5.come_ref), custom_call_target="tpu_custom_call" | custom-call | tf_op jit(solution)/shard_map/last/pallas_call | solution.py:268
  (1 shorter events, 0.0 us)
Async XLA Ops:
  0.0 1.1 %copy-start = (bf16[512,768]{1,0:T(8,128)(2,1)S(1)}, bf16[512,768]{1,0:T(8,128)(2,1)}, u32[]{:S(2)}) copy-start(bf16[512,768]{1,0:T(8,128)(2,1)} %points_ref.1) | copy-start | bytes 2359300
  0.0 1.1 %copy-start.1 = (bf16[512]{0:T(512)(128)(2,1)S(1)}, bf16[512]{0:T(512)(128)(2,1)}, u32[]{:S(2)}) copy-start(bf16[512]{0:T(512)(128)(2,1)} %pot_ref.2) | copy-start | bytes 3076
  0.0 5.8 %copy-start.2 = (bf16[4096,768]{1,0:T(8,128)(2,1)S(1)}, bf16[4096,768]{1,0:T(8,128)(2,1)}, u32[]{:S(2)}) copy-start(bf16[4096,768]{1,0:T(8,128)(2,1)} %data_ref.3) | copy-start | bytes 18874372
  0.0 5.8 %copy-start.3 = (bf16[4096]{0:T(1024)(128)(2,1)S(1)}, bf16[4096]{0:T(1024)(128)(2,1)}, u32[]{:S(2)}) copy-start(bf16[4096]{0:T(1024)(128)(2,1)} %pot_ref.3) | copy-start | bytes 24580
  1.2 17.3 %collective-permute-start.1 = (bf16[528,768]{1,0:T(8,128)(2,1)S(1)}, bf16[528,768]{1,0:T(8,128)(2,1)S(1)}, u32[]{:S(2)}, u32[]{:S(2)}) collective-permute-start(bf16[528,768]{1,0:T(8,128)(2,1)S(1)} %pack.1.query_ref), channel_id=1, source_target_pairs={{3,0},{2,1},{5,2},{4,3},{7,4},{6,5},{1,6},{0,7},{14,8},{15,9},{8,1... | collective-permute-start | bytes 2433032 | tf_op jit(solution)/shard_map/ppermute | solution.py:205
  14.4 6.3 %collective-permute-start = (f32[392,512]{1,0:T(8,128)S(1)}, f32[392,512]{1,0:T(8,128)S(1)}, u32[]{:S(2)}, u32[]{:S(2)}) collective-permute-start(f32[392,512]{1,0:T(8,128)S(1)} %get-tuple-element.19), channel_id=1, source_target_pairs={{0,8},{8,0},{16,24},{24,16},{32,40},{40,32},{48,56},{56,48},{64,72... | collective-permute-start | bytes 2408456 | tf_op jit(solution)/shard_map/ppermute | solution.py:244
  19.5 2.6 %collective-permute-start.2 = (f32[392,256]{1,0:T(8,128)S(1)}, f32[392,256]{1,0:T(8,128)S(1)}, u32[]{:S(2)}, u32[]{:S(2)}) collective-permute-start(f32[392,256]{1,0:T(8,128)S(1)} %get-tuple-element.22), channel_id=1, source_target_pairs={{0,8},{8,0},{16,24},{24,16},{32,40},{40,32},{48,56},{56,48},{64,72... | collective-permute-start | bytes 1204232 | tf_op jit(solution)/shard_map/ppermute | solution.py:257

commit v6 on v5

--- a/solution.py
+++ b/solution.py
@@ -115,28 +115,35 @@
     return pieces
 
 
-def pair_kernel(keep_u, stat_u, come_u, keep_v, stat_v, come_v, out_ref):
-    half = keep_u.shape[0]
-    merged = []
-    for keep, stat, come in ((keep_u, stat_u, come_u), (keep_v, stat_v, come_v)):
-        other = come[half:, :]
-        top = jnp.maximum(stat[0:1], other[0:1])
-        left, right = jnp.exp(stat[0:1] - top), jnp.exp(other[0:1] - top)
-        merged.append((top, stat[1:2] * left + other[1:2] * right, left, right))
-    (top_u, total_u, left_u, right_u), (top_v, total_v, left_v, right_v) = merged
-    high, middle, low = parted(top_v, 3)
-    main, rest = parted(total_v, 2)
-    tail = parted(top_u, 3) + parted(total_u, 2)
+def merged(stat, come):
+    other = come[come.shape[0] - STATS :, :]
+    top = jnp.maximum(stat[0:1], other[0:1])
+    left, right = jnp.exp(stat[0:1] - top), jnp.exp(other[0:1] - top)
+    return top, stat[1:2] * left + other[1:2] * right, left, right
+
+
+def cross_pair_kernel(keep, stat, come, out_ref, tail_ref):
+    top, total, left, right = merged(stat, come)
+    tail_ref[...] = jnp.concatenate(parted(top, 3) + parted(total, 2) + [jnp.zeros_like(top)] * 3, 0)
+    for i in range(keep.shape[0] // ROWS):
+        rows = slice(ROWS * i, ROWS * (i + 1))
+        out_ref[ORDER.index(i), :ROWS, :] = (keep[rows] * left + come[rows] * right).astype(jnp.bfloat16)
+
+
+def self_pair_kernel(keep, stat, come, tail_ref, part_ref, out_ref):
+    del part_ref
+    top, total, left, right = merged(stat, come)
+    high, middle, low = parted(top, 3)
+    main, rest = parted(total, 2)
+    tail = [tail_ref[:5, :]]
     for pieces in ((high, middle), (low, main), (rest, jnp.zeros_like(rest))):
         tail.append(jnp.concatenate(pieces, 1))
     tail = jnp.concatenate(tail, 0)
-    for i in range(half // ROWS):
+    for i in range(keep.shape[0] // ROWS):
         rows = slice(ROWS * i, ROWS * (i + 1))
-        to = ORDER.index(i)
-        out_ref[to, :ROWS, :] = (keep_u[rows] * left_u + come_u[rows] * right_u).astype(jnp.bfloat16)
-        v = keep_v[rows] * left_v + come_v[rows] * right_v
+        v = keep[rows] * left + come[rows] * right
         v = jnp.concatenate([v[: ROWS // 2], v[ROWS // 2 :]], 1)
-        out_ref[to, ROWS:, :] = jnp.concatenate([v, tail], 0).astype(jnp.bfloat16)
+        out_ref[ORDER.index(i), ROWS:, :] = jnp.concatenate([v, tail], 0).astype(jnp.bfloat16)
 
 
 def joined(parts):
@@ -242,6 +249,17 @@
         name="sums",
     )(core, weights, data, top, total)
     come_u = lax.ppermute(send_u, "dp", swap)
+    part, tail = pl.pallas_call(
+        cross_pair_kernel,
+        out_shape=[
+            jax.ShapeDtypeStruct((chips, 3 * ROWS // 2 + REST, count), jnp.bfloat16),
+            jax.ShapeDtypeStruct((STATS, count), f32),
+        ],
+        in_specs=[whole()] * 3,
+        out_specs=[whole()] * 2,
+        compiler_params=params,
+        name="cross_pair",
+    )(keep_u, stat_u, come_u)
     send_v, keep_v, stat_v = pl.pallas_call(
         self_kernel,
         out_shape=halves(count // 2),
@@ -255,16 +273,18 @@
         name="self",
     )(core, x_hi, packed, keys, stat_u)
     come_v = lax.ppermute(send_v, "dp", swap)
-    merged = pl.pallas_call(
-        pair_kernel,
-        out_shape=jax.ShapeDtypeStruct((chips, 3 * ROWS // 2 + REST, count), jnp.bfloat16),
-        in_specs=[whole()] * 6,
+    joint = jax.ShapeDtypeStruct((chips, 3 * ROWS // 2 + REST, count), jnp.bfloat16)
+    both = pl.pallas_call(
+        self_pair_kernel,
+        out_shape=joint,
+        in_specs=[whole()] * 5,
         out_specs=whole(),
-        compiler_params=params,
-        name="pair",
-    )(keep_u, stat_u, come_u, keep_v, stat_v, come_v)
+        input_output_aliases={4: 0},
+        compiler_params=params,
+        name="self_pair",
+    )(keep_v, stat_v, come_v, tail, part)
     groups = [[2 * i + k for i in ORDER] for k in range(2)]
-    come = lax.all_to_all(merged, "dp", 0, 0, axis_index_groups=groups, tiled=True)
+    come = lax.all_to_all(both, "dp", 0, 0, axis_index_groups=groups, tiled=True)
     return pl.pallas_call(
         last_kernel,
         out_shape=jax.ShapeDtypeStruct((ROWS, count), f32),

time: 37.8 us -> 37.7 us (level)
  transfers between devices with their start and end apart: 3 -> 3, of which waited for: 1 -> 1; matrix products, arithmetic and copies ran while one was open for 0% -> 0% of each run, Pallas kernels for 25% -> 26%
where the time goes in v6:
time: 37.7 us; the launch traced here: 37.4 us
  blocking collectives  14.4 us (38%)
  Pallas kernels  10.6 us (28%)
  starting transfers between devices  9.98 us (26%)
  waiting for transfers between devices  1.2 us (3%)
  local copies, waits for them, and re-layouts  1.11 us (3%)
    all_to_all x1, blocking collectives, on_device(): lax.all_to_all(both, 'dp', 0, 0, axis_index_groups=groups, tiled=True)  14.4 us
    pallas_call x1, Pallas kernels, on_device(): pl.pallas_call(weigh_kernel, out_shape=[jax.ShapeDtypeStruct((count, item...  4.82 us
    ppermute x1, starting transfers between devices, on_device(): keys = lax.ppermute(packed, ('dp', 'cores'), pairs)  4.64 us
    ppermute x1, starting transfers between devices, on_device(): come_u = lax.ppermute(send_u, 'dp', swap)  4.08 us
    pallas_call x1, Pallas kernels, on_device(): pl.pallas_call(sum_kernel, out_shape=halves(count), in_specs=[smem] + [wh...  3.63 us
    ppermute x1, starting transfers between devices, on_device(): come_v = lax.ppermute(send_v, 'dp', swap)  1.26 us
    ppermute x1, waiting for transfers between devices, on_device(): come_v = lax.ppermute(send_v, 'dp', swap)  1.19 us
    unnamed x8, local copies, waits for them, and re-layouts  1.11 us
  transfers between devices with their start and end apart: 3, of which 1 were waited for; matrix products, arithmetic and copies ran while one was open for 0% of the time, Pallas kernels for 26%

profile of v6, /device:TPU:1, one launch (start us, length us, event | category | flops | bytes accessed | tf_op | source)
XLA Modules:
  0.0 37.4 jit_solution(6979776680484904133)
XLA Ops:
  0.0 0.0 copy-start
  0.0 0.0 copy-start.1
  0.0 0.0 copy-start.2
  0.0 0.0 copy-start.3
  0.0 1.1 %copy-done = bf16[512,768]{1,0:T(8,128)(2,1)S(1)} copy-done((bf16[512,768]{1,0:T(8,128)(2,1)S(1)}, bf16[512,768]{1,0:T(8,128)(2,1)}, u32[]{:S(2)}) %copy-start) | copy-done | bytes 786456
  1.1 0.0 copy-done.1
  1.1 0.1 pack.1.query_ref
  1.2 4.6 %collective-permute-start = (bf16[528,768]{1,0:T(8,128)(2,1)S(1)}, bf16[528,768]{1,0:T(8,128)(2,1)S(1)}, u32[]{:S(2)}, u32[]{:S(2)}) collective-permute-start(bf16[528,768]{1,0:T(8,128)(2,1)S(1)} %pack.1.query_ref), channel_id=1, source_target_pairs={{3,0},{2,1},{5,2},{4,3},{7,4},{6,5},{1,6},{0,7},{14,8},{15,9},{8,1... | collective-permute-start | bytes 2433032 | tf_op jit(solution)/shard_map/ppermute | solution.py:212
  5.8 0.0 copy-done.2
  5.9 0.0 copy-done.3
  5.9 4.8 %weigh.1 = (bf16[512,4096]{1,0:T(8,128)(2,1)S(1)}, f32[512,128]{1,0:T(8,128)S(1)}, f32[512,128]{1,0:T(8,128)S(1)}) custom-call(bf16[4096]{0:T(1024)(128)(2,1)S(1)} %copy-done.3, bf16[528,768]{1,0:T(8,128)(2,1)S(1)} %pack.1.query_ref, bf16[4096,768]{1,0:T(8,128)(2,1)S(1)} %copy-done.2), custom_call_target="tpu_custom_call" | custom-call | flops 3221225472 | bytes 6291456 | tf_op jit(solution)/shard_map/weigh/pallas_call | solution.py:214
  10.7 3.6 %sums.1 = (f32[392,512]{1,0:T(8,128)S(1)}, f32[384,512]{1,0:T(8,128)S(1)}, f32[8,512]{1,0:T(8,128)S(1)}) custom-call(s32[1]{0:T(128)} %bitcast.core_ref, bf16[512,4096]{1,0:T(8,128)(2,1)S(1)} %get-tuple-element.16.weights_ref, bf16[4096,768]{1,0:T(8,128)(2,1)S(1)} %copy-done.2, f32[512,128]{1,0:T(8,128)S(1)} %get-tuple-element.17.top_ref, ...), custom_call_target="tpu_custom_call" | custom-call | flops 3221225472 | bytes 6291456 | tf_op jit(solution)/shard_map/sums/pallas_call | solution.py:239
  14.3 4.1 %collective-permute-start.2 = (f32[392,512]{1,0:T(8,128)S(1)}, f32[392,512]{1,0:T(8,128)S(1)}, u32[]{:S(2)}, u32[]{:S(2)}) collective-permute-start(f32[392,512]{1,0:T(8,128)S(1)} %get-tuple-element.24), channel_id=1, source_target_pairs={{0,8},{8,0},{16,24},{24,16},{32,40},{40,32},{48,56},{56,48},{64,72... | collective-permute-start | bytes 2408456 | tf_op jit(solution)/shard_map/ppermute | solution.py:251
  18.4 0.0 collective-permute-done.key_ref
  18.4 1.0 %self.1 = (f32[392,256]{1,0:T(8,128)S(1)}, f32[384,256]{1,0:T(8,128)S(1)}, f32[8,256]{1,0:T(8,128)S(1)}) custom-call(s32[1]{0:T(128)} %bitcast.core_ref, s32[1]{0:T(128)} %bitcast.1.half_ref, bf16[528,768]{1,0:T(8,128)(2,1)S(1)} %pack.1.query_ref, bf16[528,768]{1,0:T(8,128)(2,1)S(1)} %collective-permute-done.key_ref, ...), custom_call_target="tpu_custom_call" | custom-call | flops 402653184 | bytes 1572864 | tf_op jit(solution)/shard_map/self/pallas_call | solution.py:263
  19.4 1.3 %collective-permute-start.1 = (f32[392,256]{1,0:T(8,128)S(1)}, f32[392,256]{1,0:T(8,128)S(1)}, u32[]{:S(2)}, u32[]{:S(2)}) collective-permute-start(f32[392,256]{1,0:T(8,128)S(1)} %get-tuple-element.22), channel_id=1, source_target_pairs={{0,8},{8,0},{16,24},{24,16},{32,40},{40,32},{48,56},{56,48},{64,72... | collective-permute-start | bytes 1204232 | tf_op jit(solution)/shard_map/ppermute | solution.py:275
  20.7 0.0 collective-permute-done.2.come
  20.7 0.2 cross_pair.1
  20.8 1.2 %collective-permute-done.1.come = f32[392,256]{1,0:T(8,128)S(1)} collective-permute-done((f32[392,256]{1,0:T(8,128)S(1)}, f32[392,256]{1,0:T(8,128)S(1)}, u32[]{:S(2)}, u32[]{:S(2)}) %collective-permute-start.1) | collective-permute-done | bytes 401440 | tf_op jit(solution)/shard_map/ppermute | solution.py:275
  22.0 0.1 self_pair.1
  22.1 14.4 %all_to_all.5.come_ref = bf16[8,80,512]{2,1,0:T(8,128)(2,1)S(1)} all-to-all(bf16[8,80,512]{2,1,0:T(8,128)(2,1)S(1)} %self_pair.1), channel_id=1, replica_groups={{96,80,64,112,32,16,0,48},{104,88,72,120,40,24,8,56},{97,81,65,113,33,1..., dimensions={0} | all-to-all | bytes 1310720 | tf_op jit(solution)/shard_map/all_to_all | solution.py:287
  36.5 0.8 %last.1 = f32[48,512]{1,0:T(8,128)} custom-call(bf16[8,80,512]{2,1,0:T(8,128)(2,1)S(1)} %all_to_all.5.come_ref), custom_call_target="tpu_custom_call" | custom-call | tf_op jit(solution)/shard_map/last/pallas_call | solution.py:288
  (1 shorter events, 0.0 us)
Async XLA Ops:
  0.0 1.1 %copy-start = (bf16[512,768]{1,0:T(8,128)(2,1)S(1)}, bf16[512,768]{1,0:T(8,128)(2,1)}, u32[]{:S(2)}) copy-start(bf16[512,768]{1,0:T(8,128)(2,1)} %points_ref.1) | copy-start | bytes 2359300
  0.0 1.1 %copy-start.1 = (bf16[512]{0:T(512)(128)(2,1)S(1)}, bf16[512]{0:T(512)(128)(2,1)}, u32[]{:S(2)}) copy-start(bf16[512]{0:T(512)(128)(2,1)} %pot_ref.2) | copy-start | bytes 3076
  0.0 5.8 %copy-start.2 = (bf16[4096,768]{1,0:T(8,128)(2,1)S(1)}, bf16[4096,768]{1,0:T(8,128)(2,1)}, u32[]{:S(2)}) copy-start(bf16[4096,768]{1,0:T(8,128)(2,1)} %data_ref.3) | copy-start | bytes 18874372
  0.0 5.8 %copy-start.3 = (bf16[4096]{0:T(1024)(128)(2,1)S(1)}, bf16[4096]{0:T(1024)(128)(2,1)}, u32[]{:S(2)}) copy-start(bf16[4096]{0:T(1024)(128)(2,1)} %pot_ref.3) | copy-start | bytes 24580
  1.2 17.2 %collective-permute-start = (bf16[528,768]{1,0:T(8,128)(2,1)S(1)}, bf16[528,768]{1,0:T(8,128)(2,1)S(1)}, u32[]{:S(2)}, u32[]{:S(2)}) collective-permute-start(bf16[528,768]{1,0:T(8,128)(2,1)S(1)} %pack.1.query_ref), channel_id=1, source_target_pairs={{3,0},{2,1},{5,2},{4,3},{7,4},{6,5},{1,6},{0,7},{14,8},{15,9},{8,1... | collective-permute-start | bytes 2433032 | tf_op jit(solution)/shard_map/ppermute | solution.py:212
  14.3 6.3 %collective-permute-start.2 = (f32[392,512]{1,0:T(8,128)S(1)}, f32[392,512]{1,0:T(8,128)S(1)}, u32[]{:S(2)}, u32[]{:S(2)}) collective-permute-start(f32[392,512]{1,0:T(8,128)S(1)} %get-tuple-element.24), channel_id=1, source_target_pairs={{0,8},{8,0},{16,24},{24,16},{32,40},{40,32},{48,56},{56,48},{64,72... | collective-permute-start | bytes 2408456 | tf_op jit(solution)/shard_map/ppermute | solution.py:251
  19.4 2.6 %collective-permute-start.1 = (f32[392,256]{1,0:T(8,128)S(1)}, f32[392,256]{1,0:T(8,128)S(1)}, u32[]{:S(2)}, u32[]{:S(2)}) collective-permute-start(f32[392,256]{1,0:T(8,128)S(1)} %get-tuple-element.22), channel_id=1, source_target_pairs={{0,8},{8,0},{16,24},{24,16},{32,40},{40,32},{48,56},{56,48},{64,72... | collective-permute-start | bytes 1204232 | tf_op jit(solution)/shard_map/ppermute | solution.py:275

commit v7 on v6

--- a/solution.py
+++ b/solution.py
@@ -15,7 +15,7 @@
 WHENCE = (((1, 1), (3, 0)), ((1, 0), (3, 1)), ((0, 1), (2, 0)), ((0, 0), (2, 1)))
 VMEM_LIMIT = 16 * 2**20
 
-ORDER = (6, 5, 4, 7, 2, 1, 0, 3)
+ORDER = (6, 2, 5, 1, 4, 0, 7, 3)
 
 
 def whole():

time: 37.7 us -> 37.5 us (level)
  no operation moved by 1% of the time
where the time goes in v7:
time: 37.5 us; the launch traced here: 37.3 us
  blocking collectives  14.4 us (38%)
  Pallas kernels  10.6 us (28%)
  starting transfers between devices  9.98 us (27%)
  waiting for transfers between devices  1.2 us (3%)
  local copies, waits for them, and re-layouts  1.11 us (3%)
    all_to_all x1, blocking collectives, on_device(): lax.all_to_all(both, 'dp', 0, 0, axis_index_groups=groups, tiled=True)  14.4 us
    pallas_call x1, Pallas kernels, on_device(): pl.pallas_call(weigh_kernel, out_shape=[jax.ShapeDtypeStruct((count, item...  4.82 us
    ppermute x1, starting transfers between devices, on_device(): keys = lax.ppermute(packed, ('dp', 'cores'), pairs)  4.64 us
    ppermute x1, starting transfers between devices, on_device(): come_u = lax.ppermute(send_u, 'dp', swap)  4.08 us
    pallas_call x1, Pallas kernels, on_device(): pl.pallas_call(sum_kernel, out_shape=halves(count), in_specs=[smem] + [wh...  3.63 us
    ppermute x1, starting transfers between devices, on_device(): come_v = lax.ppermute(send_v, 'dp', swap)  1.26 us
    ppermute x1, waiting for transfers between devices, on_device(): come_v = lax.ppermute(send_v, 'dp', swap)  1.19 us
    unnamed x8, local copies, waits for them, and re-layouts  1.11 us
  transfers between devices with their start and end apart: 3, of which 1 were waited for; matrix products, arithmetic and copies ran while one was open for 0% of the time, Pallas kernels for 26%

profile of v7, /device:TPU:1, one launch (start us, length us, event | category | flops | bytes accessed | tf_op | source)
XLA Modules:
  0.0 37.3 jit_solution(5452453001727931190)
XLA Ops:
  0.0 0.0 copy-start
  0.0 0.0 copy-start.1
  0.0 0.0 copy-start.2
  0.0 0.0 copy-start.3
  0.0 1.1 %copy-done = bf16[512,768]{1,0:T(8,128)(2,1)S(1)} copy-done((bf16[512,768]{1,0:T(8,128)(2,1)S(1)}, bf16[512,768]{1,0:T(8,128)(2,1)}, u32[]{:S(2)}) %copy-start) | copy-done | bytes 786456
  1.1 0.0 copy-done.1
  1.1 0.1 pack.1.query_ref
  1.2 4.6 %collective-permute-start = (bf16[528,768]{1,0:T(8,128)(2,1)S(1)}, bf16[528,768]{1,0:T(8,128)(2,1)S(1)}, u32[]{:S(2)}, u32[]{:S(2)}) collective-permute-start(bf16[528,768]{1,0:T(8,128)(2,1)S(1)} %pack.1.query_ref), channel_id=1, source_target_pairs={{3,0},{2,1},{5,2},{4,3},{7,4},{6,5},{1,6},{0,7},{14,8},{15,9},{8,1... | collective-permute-start | bytes 2433032 | tf_op jit(solution)/shard_map/ppermute | solution.py:212
  5.8 0.0 copy-done.2
  5.9 0.0 copy-done.3
  5.9 4.8 %weigh.1 = (bf16[512,4096]{1,0:T(8,128)(2,1)S(1)}, f32[512,128]{1,0:T(8,128)S(1)}, f32[512,128]{1,0:T(8,128)S(1)}) custom-call(bf16[4096]{0:T(1024)(128)(2,1)S(1)} %copy-done.3, bf16[528,768]{1,0:T(8,128)(2,1)S(1)} %pack.1.query_ref, bf16[4096,768]{1,0:T(8,128)(2,1)S(1)} %copy-done.2), custom_call_target="tpu_custom_call" | custom-call | flops 3221225472 | bytes 6291456 | tf_op jit(solution)/shard_map/weigh/pallas_call | solution.py:214
  10.7 3.6 %sums.1 = (f32[392,512]{1,0:T(8,128)S(1)}, f32[384,512]{1,0:T(8,128)S(1)}, f32[8,512]{1,0:T(8,128)S(1)}) custom-call(s32[1]{0:T(128)} %bitcast.core_ref, bf16[512,4096]{1,0:T(8,128)(2,1)S(1)} %get-tuple-element.16.weights_ref, bf16[4096,768]{1,0:T(8,128)(2,1)S(1)} %copy-done.2, f32[512,128]{1,0:T(8,128)S(1)} %get-tuple-element.17.top_ref, ...), custom_call_target="tpu_custom_call" | custom-call | flops 3221225472 | bytes 6291456 | tf_op jit(solution)/shard_map/sums/pallas_call | solution.py:239
  14.3 4.1 %collective-permute-start.2 = (f32[392,512]{1,0:T(8,128)S(1)}, f32[392,512]{1,0:T(8,128)S(1)}, u32[]{:S(2)}, u32[]{:S(2)}) collective-permute-start(f32[392,512]{1,0:T(8,128)S(1)} %get-tuple-element.24), channel_id=1, source_target_pairs={{0,8},{8,0},{16,24},{24,16},{32,40},{40,32},{48,56},{56,48},{64,72... | collective-permute-start | bytes 2408456 | tf_op jit(solution)/shard_map/ppermute | solution.py:251
  18.4 0.0 collective-permute-done.key_ref
  18.4 1.0 %self.1 = (f32[392,256]{1,0:T(8,128)S(1)}, f32[384,256]{1,0:T(8,128)S(1)}, f32[8,256]{1,0:T(8,128)S(1)}) custom-call(s32[1]{0:T(128)} %bitcast.core_ref, s32[1]{0:T(128)} %bitcast.1.half_ref, bf16[528,768]{1,0:T(8,128)(2,1)S(1)} %pack.1.query_ref, bf16[528,768]{1,0:T(8,128)(2,1)S(1)} %collective-permute-done.key_ref, ...), custom_call_target="tpu_custom_call" | custom-call | flops 402653184 | bytes 1572864 | tf_op jit(solution)/shard_map/self/pallas_call | solution.py:263
  19.4 1.3 %collective-permute-start.1 = (f32[392,256]{1,0:T(8,128)S(1)}, f32[392,256]{1,0:T(8,128)S(1)}, u32[]{:S(2)}, u32[]{:S(2)}) collective-permute-start(f32[392,256]{1,0:T(8,128)S(1)} %get-tuple-element.22), channel_id=1, source_target_pairs={{0,8},{8,0},{16,24},{24,16},{32,40},{40,32},{48,56},{56,48},{64,72... | collective-permute-start | bytes 1204232 | tf_op jit(solution)/shard_map/ppermute | solution.py:275
  20.7 0.0 collective-permute-done.2.come
  20.7 0.2 cross_pair.1
  20.8 1.2 %collective-permute-done.1.come = f32[392,256]{1,0:T(8,128)S(1)} collective-permute-done((f32[392,256]{1,0:T(8,128)S(1)}, f32[392,256]{1,0:T(8,128)S(1)}, u32[]{:S(2)}, u32[]{:S(2)}) %collective-permute-start.1) | collective-permute-done | bytes 401440 | tf_op jit(solution)/shard_map/ppermute | solution.py:275
  22.0 0.1 self_pair.1
  22.1 14.4 %all_to_all.5.come_ref = bf16[8,80,512]{2,1,0:T(8,128)(2,1)S(1)} all-to-all(bf16[8,80,512]{2,1,0:T(8,128)(2,1)S(1)} %self_pair.1), channel_id=1, replica_groups={{96,32,80,16,64,0,112,48},{104,40,88,24,72,8,120,56},{97,33,81,17,65,1,..., dimensions={0} | all-to-all | bytes 1310720 | tf_op jit(solution)/shard_map/all_to_all | solution.py:287
  36.5 0.8 %last.1 = f32[48,512]{1,0:T(8,128)} custom-call(bf16[8,80,512]{2,1,0:T(8,128)(2,1)S(1)} %all_to_all.5.come_ref), custom_call_target="tpu_custom_call" | custom-call | tf_op jit(solution)/shard_map/last/pallas_call | solution.py:288
  (1 shorter events, 0.0 us)
Async XLA Ops:
  0.0 1.1 %copy-start = (bf16[512,768]{1,0:T(8,128)(2,1)S(1)}, bf16[512,768]{1,0:T(8,128)(2,1)}, u32[]{:S(2)}) copy-start(bf16[512,768]{1,0:T(8,128)(2,1)} %points_ref.1) | copy-start | bytes 2359300
  0.0 1.1 %copy-start.1 = (bf16[512]{0:T(512)(128)(2,1)S(1)}, bf16[512]{0:T(512)(128)(2,1)}, u32[]{:S(2)}) copy-start(bf16[512]{0:T(512)(128)(2,1)} %pot_ref.2) | copy-start | bytes 3076
  0.0 5.8 %copy-start.2 = (bf16[4096,768]{1,0:T(8,128)(2,1)S(1)}, bf16[4096,768]{1,0:T(8,128)(2,1)}, u32[]{:S(2)}) copy-start(bf16[4096,768]{1,0:T(8,128)(2,1)} %data_ref.3) | copy-start | bytes 18874372
  0.0 5.8 %copy-start.3 = (bf16[4096]{0:T(1024)(128)(2,1)S(1)}, bf16[4096]{0:T(1024)(128)(2,1)}, u32[]{:S(2)}) copy-start(bf16[4096]{0:T(1024)(128)(2,1)} %pot_ref.3) | copy-start | bytes 24580
  1.2 17.2 %collective-permute-start = (bf16[528,768]{1,0:T(8,128)(2,1)S(1)}, bf16[528,768]{1,0:T(8,128)(2,1)S(1)}, u32[]{:S(2)}, u32[]{:S(2)}) collective-permute-start(bf16[528,768]{1,0:T(8,128)(2,1)S(1)} %pack.1.query_ref), channel_id=1, source_target_pairs={{3,0},{2,1},{5,2},{4,3},{7,4},{6,5},{1,6},{0,7},{14,8},{15,9},{8,1... | collective-permute-start | bytes 2433032 | tf_op jit(solution)/shard_map/ppermute | solution.py:212
  14.3 6.3 %collective-permute-start.2 = (f32[392,512]{1,0:T(8,128)S(1)}, f32[392,512]{1,0:T(8,128)S(1)}, u32[]{:S(2)}, u32[]{:S(2)}) collective-permute-start(f32[392,512]{1,0:T(8,128)S(1)} %get-tuple-element.24), channel_id=1, source_target_pairs={{0,8},{8,0},{16,24},{24,16},{32,40},{40,32},{48,56},{56,48},{64,72... | collective-permute-start | bytes 2408456 | tf_op jit(solution)/shard_map/ppermute | solution.py:251
  19.4 2.6 %collective-permute-start.1 = (f32[392,256]{1,0:T(8,128)S(1)}, f32[392,256]{1,0:T(8,128)S(1)}, u32[]{:S(2)}, u32[]{:S(2)}) collective-permute-start(f32[392,256]{1,0:T(8,128)S(1)} %get-tuple-element.22), channel_id=1, source_target_pairs={{0,8},{8,0},{16,24},{24,16},{32,40},{40,32},{48,56},{56,48},{64,72... | collective-permute-start | bytes 1204232 | tf_op jit(solution)/shard_map/ppermute | solution.py:275
